TPU v7x, 32 devices: a whole 2x2x4 slice. The times are simulated.
32 devices in a mesh: seq: 8 (over z, y), batch: 4 (over x, core).
Axes of the slice: x: 2, y: 2, z: 4, core: 2. Of those that a mesh axis runs over, the one named last changes fastest.
Arguments:
- inputs: bfloat16 [32, 1024, 512], P('batch', 'seq'), may hold values from -6 to 6
- cotangent: bfloat16 [32, 1024, 512], P('batch', 'seq'), may hold values from -6 to 6
- lengths: int32 [32], P('batch'), may hold values from 256 to 1024, as said below
- norm1_gain: float32 [512], replicated, may hold values from 0.25 to 1.75
- norm1_bias: float32 [512], replicated, may hold values from -4 to 4
- qkv_weight: bfloat16 [512, 1536], replicated, may hold values from -0.25 to 0.25
- blend_weights: float32 [3, 8], replicated, may hold values from 0.5 to 4
- out_weight: bfloat16 [512, 512], replicated, may hold values from -1 to 1
- norm2_gain: float32 [512], replicated, may hold values from 0.25 to 1.75
- norm2_bias: float32 [512], replicated, may hold values from -4 to 4
- in_weight: bfloat16 [512, 2048], replicated, may hold values from -0.25 to 0.25
- in_bias: float32 [2048], replicated, may hold values from -4 to 4
- down_weight: bfloat16 [2048, 512], replicated, may hold values from -0.125 to 0.125
- down_bias: float32 [512], replicated, may hold values from -4 to 4
Outputs:
- output: bfloat16 [32, 1024, 512], P('batch', 'seq')
- input_grad: bfloat16 [32, 1024, 512], P('batch', 'seq')
- norm1_gain_grad: float32 [512], replicated
- norm1_bias_grad: float32 [512], replicated
- qkv_weight_grad: float32 [512, 1536], replicated
- blend_grad: float32 [3, 8], replicated
- out_weight_grad: float32 [512, 512], replicated
- norm2_gain_grad: float32 [512], replicated
- norm2_bias_grad: float32 [512], replicated
- in_weight_grad: float32 [512, 2048], replicated
- in_bias_grad: float32 [2048], replicated
- down_weight_grad: float32 [2048, 512], replicated
- down_bias_grad: float32 [512], replicated
Inputs may be any that keep to these rules, and one draw needn't show every extreme that they name: `lengths`: in each aligned group of 8 sequences one, drawn from the seed, has length 1024.
All inputs are finite; a program needn't handle non-finite values.
Results may differ from a plain program's by a relative error of at most 0.009.
Values may be sent and summed in bfloat16 or wider, within the bound.
No kernel may reach another device: no remote copies, remote signals or barrier semaphores. Data moves between devices by JAX's collectives and lax.ppermute only.
A program may use at most 320 MiB of HBM per device.

v0:
```python
import functools

import jax
import jax.numpy as jnp
from jax import lax
from jax.experimental import pallas as pl
from jax.experimental.pallas import tpu as pltpu
from jax.sharding import PartitionSpec as P

WINDOW = 30
HEAD = 64
PAIR = 2 * HEAD
TILE = 64
EPS = 1e-05
NEG = -1e30
BF16 = jnp.bfloat16
F32 = jnp.float32


def layer_norm(field, gain, shift):
    center = field - jnp.mean(field, axis=-1, keepdims=True)
    spread = jnp.mean(center * center, axis=-1, keepdims=True)
    return center * lax.rsqrt(spread + EPS) * gain + shift


def rows_product(left, right):
    return lax.dot_general(
        left, right, (((0,), (0,)), ((), ())), preferred_element_type=F32
    )


def times_transposed(left, right):
    return lax.dot_general(
        left, right, (((1,), (1,)), ((), ())), preferred_element_type=F32
    )


def times(left, right):
    return lax.dot_general(
        left, right, (((1,), (0,)), ((), ())), preferred_element_type=F32
    )


def elu_feature(field):
    return jnp.where(field > 0, field + 1.0, jnp.exp(jnp.minimum(field, 0.0)))


def tanh_feature(field):
    return 1.0 + jnp.tanh(field)


def pair_lanes(p, part=0, width=PAIR):
    return slice(p * width + part * PAIR, p * width + (part + 1) * PAIR)


def store_split(ref, index, rows, block):
    lane = lax.broadcasted_iota(jnp.int32, (block.shape[0], PAIR), 1)
    for p in range(block.shape[1] // PAIR):
        pair = block[:, pair_lanes(p)]
        for h in range(2):
            mine = (lane < HEAD) if h == 0 else (lane >= HEAD)
            ref[index + (rows, pair_lanes(p, h, 2 * PAIR))] = jnp.where(mine, pair, 0.0).astype(
                BF16
            )


def load_split(ref, index, rows, p):
    return jnp.concatenate([ref[index + (rows, pair_lanes(p, h, 2 * PAIR))] for h in range(2)], 0)


def tall(block):
    return jnp.concatenate([block[:, :PAIR], block[:, PAIR:]], 0)


def fill_features(meta_ref, q_ref, k_ref, v_ref, halo_k, halo_v, keys, values, fq, fk, split):
    rows, width = q_ref.shape
    chunk = 2 * TILE
    front = pl.ds(0, TILE)
    zero = jnp.zeros((TILE, width), F32)
    store_split(keys, (), front, halo_k[...].astype(F32) * 0.125)
    store_split(values, (), front, halo_v[...].astype(F32))
    for c in range(2):
        store_split(fk, (c,), front, zero)

    def fill(step, carry):
        at = pl.multiple_of(step * chunk, chunk)
        here, there = pl.ds(at, chunk), pl.ds(at + TILE, chunk)
        q = q_ref[here, :].astype(F32)
        k = k_ref[here, :].astype(F32)
        store_split(keys, (), there, k * 0.125)
        store_split(values, (), there, v_ref[here, :].astype(F32))
        position = meta_ref[1] + at + lax.broadcasted_iota(jnp.int32, (chunk, width), 0)
        valid = position < meta_ref[0]
        for c, feature in enumerate((elu_feature, tanh_feature)):
            if split:
                store_split(fq, (c,), here, feature(q))
            else:
                fq[c, here, :] = feature(q).astype(BF16)
            store_split(fk, (c,), there, jnp.where(valid, feature(k), 0.0))
        return carry

    lax.fori_loop(0, rows // chunk, fill, 0)


def tile_masks(meta_ref, tile):
    shape = (TILE, 2 * PAIR)
    row = lax.broadcasted_iota(jnp.int32, shape, 0)
    lane = lax.broadcasted_iota(jnp.int32, shape, 1) % PAIR
    back = row + TILE - lane
    key = meta_ref[1] + (tile - 1) * TILE + lane
    known = (key >= 0) & (key < meta_ref[0])
    near = (back >= 0) & (back <= WINDOW) & (known | (back == 0))
    return near, back >= 0


def softmax_pair(scores):
    halves = []
    for h in range(2):
        part = scores[:, h * PAIR : (h + 1) * PAIR]
        part = jnp.exp(part - jnp.max(part, axis=1, keepdims=True))
        halves.append(part * (1.0 / jnp.sum(part, axis=1, keepdims=True)))
    return jnp.concatenate(halves, 1)


def tile_constants():
    row = lax.broadcasted_iota(jnp.int32, (2 * PAIR, PAIR), 0)
    lane = lax.broadcasted_iota(jnp.int32, (2 * PAIR, PAIR), 1)
    ones = jnp.where(row // PAIR == lane // HEAD, 1.0, 0.0).astype(BF16)
    row = lax.broadcasted_iota(jnp.int32, (PAIR, 2 * PAIR), 0)
    lane = lax.broadcasted_iota(jnp.int32, (PAIR, 2 * PAIR), 1)
    return ones, row // HEAD == (lane % PAIR) // HEAD


def whole(split):
    half = split.shape[0] // 2
    return split[:half] + split[half:]


def state_share(block, fks, vs):
    ones = jnp.ones((TILE, PAIR), BF16)
    share = rows_product(whole(fks), jnp.concatenate([whole(vs), ones], 1))
    return jnp.where(block, share, 0.0)


def attend_kernel(
    meta_ref, blend_ref, q_ref, k_ref, v_ref, halo_k, halo_v, state_ref, att_ref, total_ref,
    keys, values, fq, fk, state,
):
    rows, width = q_ref.shape
    pairs = range(width // PAIR)
    fill_features(meta_ref, q_ref, k_ref, v_ref, halo_k, halo_v, keys, values, fq, fk, False)
    state[...] = state_ref[...]
    ones, block = tile_constants()

    def step(tile, carry):
        at = pl.multiple_of(tile * TILE, TILE)
        here, window, past = pl.ds(at, TILE), pl.ds(at, 2 * TILE), pl.ds(at, TILE)
        near_mask, far_mask = tile_masks(meta_ref, tile)
        q = [q_ref[here, pair_lanes(p)] for p in pairs]
        feats = [[fq[c, here, pair_lanes(p)] for c in range(2)] for p in pairs]
        held = [[state[c, p] for c in range(2)] for p in pairs]
        added = [
            [
                state_share(block, load_split(fk, (c,), past, p), load_split(values, (), past, p))
                for c in range(2)
            ]
            for p in pairs
        ]
        near = [times_transposed(q[p], load_split(keys, (), window, p)) for p in pairs]
        far = [
            [times_transposed(feats[p][c], load_split(fk, (c,), window, p)) for c in range(2)]
            for p in pairs
        ]
        near = [softmax_pair(jnp.where(near_mask, n, NEG)) for n in near]
        far = [[jnp.where(far_mask, f, 0.0) for f in fs] for fs in far]
        stack = [jnp.concatenate([n] + fs, 0).astype(BF16) for n, fs in zip(near, far)]
        wide = [jnp.concatenate([load_split(values, (), window, p), ones], 1) for p in pairs]
        sums = [times(s, w) for s, w in zip(stack, wide)]
        old = [[times(feats[p][c], held[p][c].astype(BF16)) for c in range(2)] for p in pairs]
        for p in pairs:
            mixed = blend_ref[0:1, pair_lanes(p)] * sums[p][:TILE, :PAIR]
            for c in range(2):
                mine = sums[p][(c + 1) * TILE : (c + 2) * TILE] + old[p][c]
                mixed = mixed + blend_ref[c + 1 : c + 2, pair_lanes(p)] * (
                    mine[:, :PAIR] / mine[:, PAIR:]
                )
            att_ref[here, pair_lanes(p)] = mixed.astype(BF16)
        for p in pairs:
            for c in range(2):
                state[c, p] = held[p][c] + added[p][c]
        return carry

    lax.fori_loop(0, rows // TILE, step, 0)
    last = pl.ds(rows, TILE)
    for p in pairs:
        for c in range(2):
            total_ref[c, p] = state[c, p] + state_share(
                block, load_split(fk, (c,), last, p), load_split(values, (), last, p)
            )


def slopes_of(field):
    small = jnp.exp(jnp.minimum(field, 0.0))
    bent = jnp.tanh(field)
    return [jnp.where(field > 0, 1.0, small), 1.0 - bent * bent]


def split_heads(block):
    lane = lax.broadcasted_iota(jnp.int32, block.shape, 1)
    zero = jnp.zeros_like(block)
    return jnp.concatenate(
        [jnp.where(lane < HEAD, block, zero), jnp.where(lane < HEAD, zero, block)], 0
    )


def attend_back_kernel(
    together, meta_ref, blend_ref, q_ref, k_ref, v_ref, halo_k, halo_v, state_ref, later_ref,
    go_ref, gq_ref, gk_ref, gv_ref, hk_ref, hv_ref, mix_ref, total_ref,
    keys, values, fq, fk, state, gk, gv, gfk, gon,
):
    rows, width = q_ref.shape
    pairs = range(width // PAIR)
    tiles = rows // TILE
    near_by = range(together)
    units = [(s, p) for s in near_by for p in pairs]
    fill_features(meta_ref, q_ref, k_ref, v_ref, halo_k, halo_v, keys, values, fq, fk, True)
    state[...] = state_ref[...]
    mix_ref[...] = jnp.zeros_like(mix_ref)
    gk[:TILE, :] = jnp.zeros((TILE, width), F32)
    gv[:TILE, :] = jnp.zeros((TILE, width), F32)
    gfk[:, :TILE, :] = jnp.zeros((2, TILE, width), F32)
    ones, block = tile_constants()
    row = lax.broadcasted_iota(jnp.int32, (2 * PAIR, PAIR), 0) % PAIR
    lane = lax.broadcasted_iota(jnp.int32, (2 * PAIR, PAIR), 1)
    heads = jnp.where(row // HEAD == lane // HEAD, 1.0, 0.0).astype(BF16)
    plain_ones = jnp.ones((TILE, PAIR), BF16)
    high = (lax.broadcasted_iota(jnp.int32, (TILE, PAIR), 1) % HEAD) < HEAD // 2

    def step(number, carry):
        first = number * together
        at = pl.multiple_of(first * TILE, TILE)
        here = [pl.ds(at + s * TILE, TILE) for s in range(together + 1)]
        window = [pl.ds(at + s * TILE, 2 * TILE) for s in near_by]
        masks = [tile_masks(meta_ref, first + s) for s in near_by]
        q = {(s, p): q_ref[here[s], pair_lanes(p)] for s, p in units}
        go = {(s, p): go_ref[here[s], pair_lanes(p)] for s, p in units}
        blend = [[blend_ref[c : c + 1, pair_lanes(p)] for c in range(3)] for p in pairs]
        fqs = {(s, p): [load_split(fq, (c,), here[s], p) for c in range(2)] for s, p in units}
        feats = {u: [whole(f) for f in fqs[u]] for u in units}
        ks = {(s, p): load_split(keys, (), window[s], p) for s, p in units}
        fks = {(s, p): [load_split(fk, (c,), window[s], p) for c in range(2)] for s, p in units}
        wide = {
            (s, p): jnp.concatenate([load_split(values, (), window[s], p), ones], 1)
            for s, p in units
        }
        held = {(0, p): [state[c, p] for c in range(2)] for p in pairs}
        for s, p in units:
            vs = load_split(values, (), here[s], p)
            held[s + 1, p] = [
                held[s, p][c] + state_share(block, load_split(fk, (c,), here[s], p), vs)
                for c in range(2)
            ]
        past = {u: [h.astype(BF16) for h in held[u]] for u in units}
        old_k = [gk[here[0], pair_lanes(p)] for p in pairs]
        old_v = [gv[here[0], pair_lanes(p)] for p in pairs]
        old_f = [[gfk[c, here[0], pair_lanes(p)] for c in range(2)] for p in pairs]

        near = {u: times_transposed(q[u], ks[u]) for u in units}
        far = {u: [times_transposed(feats[u][c], fks[u][c]) for c in range(2)] for u in units}
        old = {u: [times(feats[u][c], past[u][c]) for c in range(2)] for u in units}
        near = {u: softmax_pair(jnp.where(masks[u[0]][0], near[u], NEG)) for u in units}
        far = {u: [jnp.where(masks[u[0]][1], f, 0.0).astype(BF16) for f in far[u]] for u in units}
        stack = {u: jnp.concatenate([near[u].astype(BF16)] + far[u], 0) for u in units}
        sums = {u: times(stack[u], wide[u]) for u in units}
        scales, prods = {}, {}
        for u in units:
            outs = [sums[u][:TILE, :PAIR]]
            scales[u] = [jnp.broadcast_to(blend[u[1]][0], (TILE, PAIR))]
            for c in range(2):
                mine = sums[u][(c + 1) * TILE : (c + 2) * TILE] + old[u][c]
                inverse = 1.0 / mine[:, PAIR:]
                outs.append(mine[:, :PAIR] * inverse)
                scales[u].append(blend[u[1]][c + 1] * inverse)
            prods[u] = jnp.concatenate([go[u] * out for out in outs], 0)
        deltas = {}
        for u in units:
            low = prods[u].astype(BF16)
            rest = (prods[u] - low.astype(F32)).astype(BF16)
            deltas[u] = times(jnp.concatenate([low, rest], 1), heads)
        grads = {}
        for u in units:
            grads[u] = []
            for c in range(3):
                delta = scales[u][c] * deltas[u][c * TILE : (c + 1) * TILE] * (-2.0 / HEAD)
                delta_low = delta.astype(BF16).astype(F32)
                delta = jnp.where(high, delta_low, delta - delta_low)
                grads[u].append(jnp.concatenate([scales[u][c] * go[u], delta], 1).astype(BF16))
        back = {u: times_transposed(jnp.concatenate(grads[u], 0), wide[u]) for u in units}
        late = {u: [times_transposed(grads[u][c + 1], past[u][c]) for c in range(2)] for u in units}
        ds = {u: (near[u] * back[u][:TILE]).astype(BF16) for u in units}
        gas = {
            u: [
                jnp.where(masks[u[0]][1], back[u][(c + 1) * TILE : (c + 2) * TILE], 0.0).astype(BF16)
                for c in range(2)
            ]
            for u in units
        }
        gq_near = {u: times(ds[u], ks[u]) for u in units}
        gq_far = {u: [times(gas[u][c], fks[u][c]) + late[u][c] for c in range(2)] for u in units}
        new_k = {u: rows_product(tall(ds[u]), split_heads(q[u] * 0.125)) for u in units}
        new_f = {u: [rows_product(tall(gas[u][c]), fqs[u][c]) for c in range(2)] for u in units}
        new_v = {
            u: rows_product(
                jnp.concatenate([tall(stack[u][c * TILE : (c + 1) * TILE]) for c in range(3)], 0),
                jnp.concatenate([split_heads(g[:, :PAIR]) for g in grads[u]], 0),
            )
            for u in units
        }

        def overlap(old, new, p):
            parts = [old + new(0, p)[:TILE]]
            parts += [new(s, p)[TILE:] + new(s + 1, p)[:TILE] for s in range(together - 1)]
            return parts + [new(together - 1, p)[TILE:]]

        for s, p in units:
            u, lanes = (s, p), pair_lanes(p)
            slopes = slopes_of(q[u].astype(F32))
            gq = gq_near[u] + slopes[0] * gq_far[u][0] + slopes[1] * gq_far[u][1]
            gq_ref[here[s], lanes] = gq.astype(BF16)
            for c in range(2):
                gon[c, here[s], p * 2 * PAIR : (p + 1) * 2 * PAIR] = grads[u][c + 1]
        for p in pairs:
            lanes = pair_lanes(p)
            for c in range(3):
                mix_ref[c : c + 1, lanes] += sum(
                    jnp.sum(prods[s, p][c * TILE : (c + 1) * TILE], axis=0, keepdims=True)
                    for s in near_by
                )
            for rows_at, part in zip(here, overlap(old_k[p], lambda s, p: new_k[s, p], p)):
                gk[rows_at, lanes] = part
            for rows_at, part in zip(here, overlap(old_v[p], lambda s, p: new_v[s, p], p)):
                gv[rows_at, lanes] = part
            for c in range(2):
                parts = overlap(old_f[p][c], lambda s, p: new_f[s, p][c], p)
                for rows_at, part in zip(here, parts):
                    gfk[c, rows_at, lanes] = part
                state[c, p] = held[together, p][c]
        return carry

    lax.fori_loop(0, tiles // together, step, 0)
    hk_ref[...] = gk[:TILE, :].astype(BF16)
    hv_ref[...] = gv[:TILE, :].astype(BF16)
    state[...] = later_ref[...]

    def come(at, c, p):
        here = pl.ds(at, TILE)
        grads = gon[c, here, p * 2 * PAIR : (p + 1) * 2 * PAIR]
        share = rows_product(whole(load_split(fq, (c,), here, p)), grads)
        return jnp.where(block, share, 0.0)

    def back_step(number, carry):
        first = tiles - 1 - number * together
        at = [pl.multiple_of((first - s) * TILE, TILE) for s in near_by]
        here = [pl.ds(a, TILE) for a in at]
        there = [pl.ds(a + TILE, TILE) for a in at]
        held = {(-1, p): [state[c, p] for c in range(2)] for p in pairs}
        for s, p in units:
            tile = first - s + 2
            nearer = pl.multiple_of(jnp.minimum(tile, tiles - 1) * TILE, TILE)
            held[s, p] = [
                held[s - 1, p][c] + jnp.where(tile < tiles, come(nearer, c, p), 0.0)
                for c in range(2)
            ]
        later = {u: [h.astype(BF16) for h in held[u]] for u in units}
        vs = {(s, p): whole(load_split(values, (), there[s], p)) for s, p in units}
        fks = {
            (s, p): jnp.concatenate([whole(load_split(fk, (c,), there[s], p)) for c in range(2)], 1)
            for s, p in units
        }
        wide = {u: jnp.concatenate([vs[u], plain_ones], 1) for u in units}
        far_k = {u: [times_transposed(wide[u], later[u][c]) for c in range(2)] for u in units}
        far_v = {
            u: times(fks[u], jnp.concatenate([g[:, :PAIR] for g in later[u]], 0)) for u in units
        }
        for s, p in units:
            u, lanes = (s, p), pair_lanes(p)
            position = meta_ref[1] + at[s] + lax.broadcasted_iota(jnp.int32, (TILE, PAIR), 0)
            slopes = slopes_of(k_ref[here[s], lanes].astype(F32))
            grad_f = [gfk[c, there[s], lanes] + far_k[u][c] for c in range(2)]
            bent = slopes[0] * grad_f[0] + slopes[1] * grad_f[1]
            grad_k = gk[there[s], lanes] + jnp.where(position < meta_ref[0], bent, 0.0)
            gk_ref[here[s], lanes] = grad_k.astype(BF16)
            gv_ref[here[s], lanes] = (gv[there[s], lanes] + far_v[u]).astype(BF16)
        for p in pairs:
            for c in range(2):
                state[c, p] = held[together - 1, p][c]
        return carry

    lax.fori_loop(0, tiles // together, back_step, 0)
    for p in pairs:
        for c in range(2):
            total_ref[c, p] = state[c, p] + come(0, c, p) + come(TILE, c, p)


def attention_specs(rows, width, count, number, split):
    lanes, calls = width // count, count

    def columns(height, part):
        return pl.BlockSpec((height, lanes), lambda _: (0, part * calls + number))

    state = pl.BlockSpec(
        (2, lanes // PAIR, PAIR, 2 * PAIR), lambda _: (0, number, 0, 0)
    )
    ins = [pl.BlockSpec(memory_space=pltpu.SMEM), columns(3, 0)]
    ins += [columns(rows, part) for part in range(3)]
    ins += [columns(TILE, part) for part in range(2)]
    scratch = [
        pltpu.VMEM((rows + TILE, 2 * lanes), BF16),
        pltpu.VMEM((rows + TILE, 2 * lanes), BF16),
        pltpu.VMEM((2, rows, (2 if split else 1) * lanes), BF16),
        pltpu.VMEM((2, rows + TILE, 2 * lanes), BF16),
        pltpu.VMEM((2, lanes // PAIR, PAIR, 2 * PAIR), F32),
    ]
    return lanes, columns, ins, state, scratch


def outcome(shape, dtype):
    return jax.ShapeDtypeStruct(shape, dtype), pl.BlockSpec(shape, lambda _: (0,) * len(shape))


def attend(meta, blend, qkv, halo, state):
    rows, width = qkv.shape[0], qkv.shape[1] // 3
    _, _, ins, held, scratch = attention_specs(rows, width, 1, 0, False)
    shapes, blocks = zip(outcome((rows, width), BF16), outcome(state.shape, F32))
    return pl.pallas_call(
        attend_kernel,
        grid=(1,),
        out_shape=shapes,
        in_specs=ins + [held],
        out_specs=blocks,
        scratch_shapes=scratch,
        compiler_params=pltpu.CompilerParams(vmem_limit_bytes=48 * 2**20),
        cost_estimate=pl.CostEstimate(
            flops=rows * width * 48000, bytes_accessed=rows * width * 8, transcendentals=0
        ),
    )(meta, blend, qkv, qkv, qkv, halo, halo, state)


def attend_back(meta, blend, qkv, halo, state, later, go, calls, number):
    rows, width = qkv.shape[0], qkv.shape[1] // 3
    lanes, columns, ins, held, scratch = attention_specs(rows, width, calls, number, True)
    shapes, blocks = zip(
        *[outcome((rows, lanes), BF16)] * 3,
        *[outcome((TILE, lanes), BF16)] * 2,
        outcome((3, lanes), F32),
        outcome((2, lanes // PAIR, PAIR, 2 * PAIR), F32),
    )
    together = 4 * PAIR // lanes
    return pl.pallas_call(
        functools.partial(attend_back_kernel, together),
        grid=(1,),
        out_shape=shapes,
        in_specs=ins + [held, held, columns(rows, 0)],
        out_specs=blocks,
        scratch_shapes=scratch
        + [
            pltpu.VMEM((rows + TILE, lanes), F32),
            pltpu.VMEM((rows + TILE, lanes), F32),
            pltpu.VMEM((2, rows + TILE, lanes), F32),
            pltpu.VMEM((2, rows, 2 * lanes), BF16),
        ],
        compiler_params=pltpu.CompilerParams(vmem_limit_bytes=56 * 2**20),
        cost_estimate=pl.CostEstimate(
            flops=rows * lanes * 96000, bytes_accessed=rows * lanes * 16, transcendentals=0
        ),
    )(meta, blend, qkv, qkv, qkv, halo, halo, state, later, go)


CHUNK = 256
GELU_A, GELU_B = 0.7978845608028654, 0.044715


def normalized(field):
    center = field - jnp.mean(field, axis=-1, keepdims=True)
    scale = lax.rsqrt(jnp.mean(center * center, axis=-1, keepdims=True) + EPS)
    return center * scale, scale


def norm_back(grad, unit, scale):
    shared = jnp.mean(grad * unit, axis=-1, keepdims=True)
    return scale * (grad - jnp.mean(grad, axis=-1, keepdims=True) - unit * shared)


def gelu_pair(field):
    square = field * field
    bent = jnp.tanh(GELU_A * field * (1.0 + GELU_B * square))
    half = 0.5 + 0.5 * bent
    slope = half + 0.5 * field * (1.0 - bent * bent) * (GELU_A + 3.0 * GELU_A * GELU_B * square)
    return field * half, slope


def column_sum(block):
    return jnp.sum(block, axis=0, keepdims=True)


def feed_kernel(
    pieces, x_ref, att_ref, grad_ref, out_w, gain_ref, bias_ref, in_w, in_b, down_w, down_b,
    result_ref, first_ref, go_ref, packed_ref, small_ref, wide_ref,
    second, hidden, pre_low, att_low,
):
    rows, width = x_ref.shape
    inner = in_w.shape[1]
    small_ref[...] = jnp.zeros_like(small_ref)
    wide_ref[...] = jnp.zeros_like(wide_ref)

    def step(number, carry):
        here = pl.ds(pl.multiple_of(number * CHUNK, CHUNK), CHUNK)
        first = x_ref[here, :].astype(F32) + times(att_ref[here, :], out_w[...])
        unit, scale = normalized(first)
        low = (unit * gain_ref[...] + bias_ref[...]).astype(BF16)
        second[here, :] = low
        grad = grad_ref[here, :]
        grad_f = grad.astype(F32)
        result = first + down_b[...]
        back = jnp.zeros((CHUNK, width), F32)
        for at in range(0, inner, width):
            lanes = slice(at, at + width)
            act, slope = gelu_pair(times(low, in_w[:, lanes]) + in_b[:, lanes])
            act = act.astype(BF16)
            hidden[here, lanes] = act
            result = result + times(act, down_w[lanes, :])
            pre = (times_transposed(grad, down_w[lanes, :]) * slope).astype(BF16)
            pre_low[here, lanes] = pre
            wide_ref[:, lanes] += column_sum(pre.astype(F32))
            back = back + times_transposed(pre, in_w[:, lanes])
        result_ref[here, :] = result.astype(BF16)
        small_ref[0:1, :] += column_sum(back * unit)
        small_ref[1:2, :] += column_sum(back)
        small_ref[2:3, :] += column_sum(grad_f)
        grad_first = grad_f + norm_back(back * gain_ref[...], unit, scale)
        first_ref[here, :] = grad_first
        grad_att = grad_first.astype(BF16)
        att_low[here, :] = grad_att
        go_ref[here, :] = times_transposed(grad_att, out_w[...])
        return carry

    lax.fori_loop(0, rows // CHUNK, step, 0)
    for at in range(0, inner, width):
        lanes = slice(at, at + width)
        packed_ref[:, lanes] = rows_product(second[...], pre_low[:, lanes]).astype(BF16)
    packed_ref[:, inner : inner + width] = rows_product(att_ref[...], att_low[...]).astype(BF16)
    tall_rows, flat_rows = inner // pieces, width // pieces
    for at in range(0, inner, width):
        share = rows_product(hidden[:, at : at + width], grad_ref[...]).astype(BF16)
        for below in range(0, width, flat_rows):
            piece, block = divmod(at + below, tall_rows)
            lanes = inner + width + block // flat_rows * width
            packed_ref[piece * flat_rows : (piece + 1) * flat_rows, lanes : lanes + width] = share[
                below : below + flat_rows
            ]


def feed_forward(pieces, x, att, grad, out_w, gain, bias, in_w, in_b, down_w, down_b):
    rows, width = x.shape
    inner = in_w.shape[1]
    return pl.pallas_call(
        functools.partial(feed_kernel, pieces),
        out_shape=(
            jax.ShapeDtypeStruct((rows, width), BF16),
            jax.ShapeDtypeStruct((rows, width), F32),
            jax.ShapeDtypeStruct((rows, width), F32),
            jax.ShapeDtypeStruct((width, 2 * inner + width), BF16),
            jax.ShapeDtypeStruct((3, width), F32),
            jax.ShapeDtypeStruct((1, inner), F32),
        ),
        in_specs=[pl.BlockSpec(memory_space=pltpu.VMEM)] * 10,
        out_specs=(pl.BlockSpec(memory_space=pltpu.VMEM),) * 6,
        scratch_shapes=[
            pltpu.VMEM((rows, width), BF16),
            pltpu.VMEM((rows, inner), BF16),
            pltpu.VMEM((rows, inner), BF16),
            pltpu.VMEM((rows, width), BF16),
        ],
        compiler_params=pltpu.CompilerParams(vmem_limit_bytes=56 * 2**20),
        cost_estimate=pl.CostEstimate(
            flops=rows * width * inner * 24, bytes_accessed=rows * width * 20, transcendentals=0
        ),
    )(x, att, grad, out_w, gain[None], bias[None], in_w, in_b[None], down_w, down_b[None])


def project_back_kernel(
    calls, x_ref, first_ref, w_ref, gain_ref, bias_ref, mix_ref, small2_ref, wide_ref, *refs
):
    grads = refs[: 3 * calls]
    result_ref, packed_ref, normed, gathered, sums, rows_of = refs[3 * calls :]
    rows, width = x_ref.shape
    sums[...] = jnp.zeros_like(sums)

    def step(number, carry):
        here = pl.ds(pl.multiple_of(number * CHUNK, CHUNK), CHUNK)
        unit, scale = normalized(x_ref[here, :].astype(F32))
        normed[here, :] = (unit * gain_ref[...] + bias_ref[...]).astype(BF16)
        grad = jnp.concatenate([ref[here, :] for ref in grads], 1)
        gathered[here, :] = grad
        back = times_transposed(grad, w_ref[...])
        sums[0:1, :] += column_sum(back * unit)
        sums[1:2, :] += column_sum(back)
        grad_x = first_ref[here, :] + norm_back(back * gain_ref[...], unit, scale)
        result_ref[here, :] = grad_x.astype(BF16)
        return carry

    lax.fori_loop(0, rows // CHUNK, step, 0)
    for at in range(0, 3 * width, width):
        lanes = slice(at, at + width)
        packed_ref[:, lanes] = rows_product(normed[...], gathered[:, lanes]).astype(BF16)
    rows_of[...] = jnp.zeros_like(rows_of)
    at = 0
    for ref in (sums, small2_ref, mix_ref, wide_ref):
        for row in range(ref.shape[0]):
            for lane in range(0, ref.shape[1], PAIR):
                rows_of[at : at + 1, :] = ref[row : row + 1, lane : lane + PAIR]
                at += 1
    high = rows_of[...].astype(BF16)
    packed_ref[:, 3 * width : 3 * width + PAIR] = high
    packed_ref[:, 3 * width + PAIR :] = (rows_of[...] - high.astype(F32)).astype(BF16)


def project_back(x, grad_first, weight, gain, bias, mix, small2, wide, grads):
    rows, width = x.shape
    vmem = pl.BlockSpec(memory_space=pltpu.VMEM)
    return pl.pallas_call(
        functools.partial(project_back_kernel, len(grads) // 3),
        out_shape=(
            jax.ShapeDtypeStruct((rows, width), BF16),
            jax.ShapeDtypeStruct((width, 3 * width + 2 * PAIR), BF16),
        ),
        in_specs=[vmem] * (8 + len(grads)),
        out_specs=(vmem, vmem),
        scratch_shapes=[
            pltpu.VMEM((rows, width), BF16),
            pltpu.VMEM((rows, 3 * width), BF16),
            pltpu.VMEM((2, width), F32),
            pltpu.VMEM((width, PAIR), F32),
        ],
        compiler_params=pltpu.CompilerParams(vmem_limit_bytes=48 * 2**20),
        cost_estimate=pl.CostEstimate(
            flops=rows * width * width * 24, bytes_accessed=rows * width * 20, transcendentals=0
        ),
    )(x, grad_first, weight, gain[None], bias[None], mix, small2, wide, *grads)


def to_sequences(block, axis, groups):
    return lax.all_to_all(block, axis, 0, 0, axis_index_groups=groups)


def from_parts(total, axis, parts, stride, forward):
    size = lax.axis_size(axis)
    low = total.astype(BF16)
    result = jnp.zeros_like(total)
    for hop in range(1, parts):
        distance = hop * stride
        route = [
            (i, i + distance) if forward else (i + distance, i) for i in range(size - distance)
        ]
        result = result + lax.ppermute(low, axis, route).astype(F32)
    return result


class Ring:
    def __init__(self, batch, seq):
        self.batch, self.seq = batch, seq
        self.low = 2 ** ((seq.bit_length() - 1) // 2)
        self.sizes = {"core": 2, "near": batch // 2 * self.low, "far": seq // self.low}
        self.pieces = batch * seq

    def place(self, s, b):
        return {"core": b % 2, "near": b // 2 * self.low + s % self.low, "far": s // self.low}

    def device(self, place):
        s = place["far"] * self.low + place["near"] % self.low
        return s * self.batch + place["near"] // self.low * 2 + place["core"]

    def mine(self):
        return self.place(lax.axis_index("seq"), lax.axis_index("batch"))

    def swap(self, value, level, k):
        route = []
        for s in range(self.seq):
            for b in range(self.batch):
                place = self.place(s, b)
                place[level] ^= k
                route.append((s * self.batch + b, self.device(place)))
        return lax.ppermute(value, ("seq", "batch"), route)

    def scatter(self, value, level, fine):
        size, me = self.sizes[level], self.mine()[level]
        value = value.reshape((size, value.shape[0] // size) + value.shape[1:])
        parts = [
            self.swap(lax.dynamic_index_in_dim(value, me ^ k, 0, False), level, k)
            for k in range(1, size)
        ]
        total = lax.dynamic_index_in_dim(value, me, 0, False).astype(F32)
        for part in parts:
            total = total + part.astype(F32)
        if not fine:
            return total.astype(BF16)
        end = total.shape[-1] - 2 * fine
        exact = total[..., end : end + fine] + total[..., end + fine :]
        high = lax.reduce_precision(exact, 8, 7)
        return jnp.concatenate([total[..., :end], high, exact - high], -1).astype(BF16)

    def gather(self, value, level):
        parts = [value] + [self.swap(value, level, k) for k in range(1, self.sizes[level])]
        return jnp.concatenate(parts, 0)

    def reduce(self, value, fine=0):
        value = value.reshape(self.pieces, value.shape[0] // self.pieces, value.shape[1])
        for level in ("core", "near", "far"):
            value = self.scatter(value, level, fine)
        for level in ("far", "near"):
            value = self.gather(value, level)
        return value, self.swap(value, "core", 1)

    def order(self):
        me = self.mine()
        piece = jnp.arange(self.pieces, dtype=jnp.int32)
        far, near = self.sizes["far"], self.sizes["near"]
        core = (piece // (far * near)) ^ me["core"]
        near = ((piece // far) % near) ^ me["near"]
        return (core * self.sizes["near"] + near) * far + ((piece % far) ^ me["far"])


def unpack_kernel(write, order_ref, own_ref, other_ref, *out_refs):
    half = own_ref.shape[0]
    for piece in range(2 * half):
        at = order_ref[piece]

        @pl.when(at < half)
        def _(piece=piece, at=at):
            write(piece, own_ref[at].astype(F32), out_refs)

        @pl.when(at >= half)
        def _(piece=piece, at=at):
            write(piece, other_ref[at - half].astype(F32), out_refs)


def write_feed(piece, block, out_refs):
    in_ref, out_ref, down_ref = out_refs
    size, inner, width = block.shape[0], in_ref.shape[1], in_ref.shape[0]
    rows = slice(piece * size, (piece + 1) * size)
    in_ref[rows, :] = block[:, :inner]
    out_ref[rows, :] = block[:, inner : inner + width]
    tall_rows = inner // (width // size)
    for below in range(0, tall_rows, size):
        at = inner + width + below // size * width
        down_ref[piece * tall_rows + below : piece * tall_rows + below + size, :] = block[
            :, at : at + width
        ]


def write_project(piece, block, out_refs):
    w_ref, small_ref = out_refs
    size, end = block.shape[0], w_ref.shape[1]
    rows = slice(piece * size, (piece + 1) * size)
    w_ref[rows, :] = block[:, :end]
    small_ref[rows, :] = block[:, end : end + PAIR] + block[:, end + PAIR :]


def unpack(write, order, halves, shapes):
    vmem = pl.BlockSpec(memory_space=pltpu.VMEM)
    return pl.pallas_call(
        functools.partial(unpack_kernel, write),
        out_shape=[jax.ShapeDtypeStruct(shape, F32) for shape in shapes],
        in_specs=[pl.BlockSpec(memory_space=pltpu.SMEM), vmem, vmem],
        out_specs=[vmem] * len(shapes),
        compiler_params=pltpu.CompilerParams(vmem_limit_bytes=48 * 2**20),
        cost_estimate=pl.CostEstimate(
            flops=0, bytes_accessed=8 * halves[0].size, transcendentals=0
        ),
    )(order, *halves)


def local(
    inputs,
    cotangent,
    lengths,
    norm1_gain,
    norm1_bias,
    qkv_weight,
    blend_weights,
    out_weight,
    norm2_gain,
    norm2_bias,
    in_weight,
    in_bias,
    down_weight,
    down_bias,
):
    seqs, span, width = inputs.shape
    heads = blend_weights.shape[1]
    devices = lax.axis_size("seq")
    parts = devices // seqs
    rows = seqs * span
    index = lax.axis_index("seq")
    groups = None
    if parts > 1:
        groups = [[r * seqs + s for s in range(seqs)] for r in range(parts)]
    mine, part = index % seqs, index // seqs
    meta = jnp.stack([lax.dynamic_index_in_dim(lengths, mine, 0, False), part * rows])
    blend = jnp.repeat(blend_weights, width // heads, axis=1)

    ring = Ring(lax.axis_size("batch"), devices)
    by_ring = width % (16 * ring.pieces) == 0
    inner = in_weight.shape[1]

    x = to_sequences(inputs, "seq", groups).reshape(rows, width)
    grad_out = to_sequences(cotangent, "seq", groups).reshape(rows, width)

    normed = layer_norm(x.astype(F32), norm1_gain, norm1_bias).astype(BF16)
    qkv = times(normed, qkv_weight).astype(BF16)
    halo = jnp.zeros((TILE, 2 * width), BF16)
    state = jnp.zeros((2, width // PAIR, PAIR, 2 * PAIR), F32)
    later = state
    if parts > 1:
        onward = [(i, i + seqs) for i in range(devices - seqs)]
        halo = lax.ppermute(qkv[rows - TILE :, width:], "seq", onward)
        total = attend(meta, blend, qkv, halo, state)[1]
        state = from_parts(total, "seq", parts, seqs, True)
    attended = attend(meta, blend, qkv, halo, state)[0]

    result, grad_first, grad_o, feed_grads, small2, grad_in_b = feed_forward(
        ring.pieces if by_ring else 16,
        x, attended, grad_out, out_weight, norm2_gain, norm2_bias,
        in_weight, in_bias, down_weight, down_bias,
    )
    output = to_sequences(result.reshape(seqs, span, width), "seq", groups)
    if by_ring:
        feed_halves = ring.reduce(feed_grads)

    calls = 4

    def back(later):
        return [
            attend_back(meta, blend, qkv, halo, state, later, grad_o, calls, number)
            for number in range(calls)
        ]

    if parts > 1:
        total = jnp.concatenate([call[6] for call in back(later)], 1)
        later = from_parts(total, "seq", parts, seqs, False)
    backs = back(later)
    grads = [[call[part] for call in backs] for part in range(3)]
    if parts > 1:
        homeward = [(i + seqs, i) for i in range(devices - seqs)]
        for part in (1, 2):
            for number in range(calls):
                received = lax.ppermute(backs[number][part + 2], "seq", homeward)
                grad = grads[part][number]
                tail = grad[rows - TILE :].astype(F32) + received.astype(F32)
                grads[part][number] = grad.at[rows - TILE :].set(tail.astype(BF16))
    mix = jnp.concatenate([call[5] for call in backs], 1)
    grad_x, project_grads = project_back(
        x, grad_first, qkv_weight, norm1_gain, norm1_bias, mix, small2, grad_in_b,
        grads[0] + grads[1] + grads[2],
    )
    input_grad = to_sequences(grad_x.reshape(seqs, span, width), "seq", groups)

    if by_ring:
        order = ring.order()
        project_halves = ring.reduce(project_grads, PAIR)
    else:
        order = jnp.arange(16, dtype=jnp.int32)
        total = lax.psum((feed_grads.astype(F32), project_grads.astype(F32)), ("seq", "batch"))
        feed_halves, project_halves = [
            [half.reshape(8, width // 16, -1) for half in (t[: width // 2], t[width // 2 :])]
            for t in total
        ]
    grad_in_w, grad_out_w, grad_down_w = unpack(
        write_feed, order, feed_halves, [(width, inner), (width, width), (inner, width)]
    )
    grad_qkv_w, small = unpack(
        write_project, order, project_halves, [(width, 3 * width), (width, PAIR)]
    )
    vectors = small.reshape(-1)
    vector = [vectors[at : at + width] for at in range(0, 8 * width, width)]
    grad_blend = vectors[5 * width : 8 * width].reshape(3, heads, width // heads).sum(-1)
    return (
        output,
        input_grad,
        vector[0],
        vector[1],
        grad_qkv_w,
        grad_blend,
        grad_out_w,
        vector[2],
        vector[3],
        grad_in_w,
        vectors[8 * width : 8 * width + inner],
        grad_down_w,
        vector[4],
    )


def solution(mesh):
    rows = P("batch", "seq", None)
    return jax.shard_map(
        local,
        mesh=mesh,
        in_specs=(rows, rows, P("batch")) + (P(),) * 11,
        out_specs=(rows, rows) + (P(),) * 11,
        check_vma=False,
    )
```

profile of v0, /device:TPU:0, one launch (start us, length us, event | category | flops | bytes accessed | tf_op | source)
XLA Modules:
  0.0 332.9 jit_solution(18340223480070560867)
XLA Ops:
  0.6 7.3 %all-to-all-start = ((bf16[8,128,512]{2,1,0:T(8,128)(2,1)}), bf16[8,128,512]{2,1,0:T(8,128)(2,1)S(1)}, u32[]{:S(2)}, u32[]{:S(2)}) async-start(bf16[8,128,512]{2,1,0:T(8,128)(2,1)} %param.14), calls=%async_computation | async-start | bytes 2097152 | tf_op jit(solution)/shard_map/all_to_all | solution.py:653
  10.8 22.9 %all-to-all-done = bf16[8,128,512]{2,1,0:T(8,128)(2,1)S(1)} async-done(((bf16[8,128,512]{2,1,0:T(8,128)(2,1)}), bf16[8,128,512]{2,1,0:T(8,128)(2,1)S(1)}, u32[]{:S(2)}, u32[]{:S(2)}) %all-to-all-start) | async-done | bytes 1048608 | tf_op jit(solution)/shard_map/all_to_all | solution.py:653
  33.7 3.6 %all-to-all-start.1 = ((bf16[8,128,512]{2,1,0:T(8,128)(2,1)}), bf16[8,128,512]{2,1,0:T(8,128)(2,1)S(1)}, u32[]{:S(2)}, u32[]{:S(2)}) async-start(bf16[8,128,512]{2,1,0:T(8,128)(2,1)} %param.15), calls=%async_computation.1 | async-start | bytes 2097152 | tf_op jit(solution)/shard_map/all_to_all | solution.py:653
  38.1 5.0 %convolution_convert_fusion.q_ref.k_ref.v_ref = bf16[1024,1536]{1,0:T(8,128)(2,1)} fusion(bf16[512,1536]{1,0:T(8,128)(2,1)} %w_ref.1, bf16[1024,512]{1,0:T(8,128)(2,1)S(1)} %bitcast.62, f32[512]{0:T(512)S(1)} %copy-done.5, f32[512]{0:T(512)S(1)} %copy-done.6, f32[1024]{0:T(1024)S(1)} %rsqrt_bitcast_fusion, f32[1024]{0:T(1024)S(1)} %get-tuple-element.100), kind=kOutput, calls=%fused_computation.2 | convolution fusion | flops 1615331328 | bytes 5779456 | tf_op jit(solution)/shard_map/dot_general | solution.py:39
  43.2 22.2 %shard_map.237 = (bf16[1024,512]{1,0:T(8,128)(2,1)S(1)}, f32[2,4,128,256]{3,2,1,0:T(8,128)}) custom-call(s32[2]{0:T(128)S(1)} %pad_add_fusion.meta_ref, f32[3,512]{1,0:T(4,128)S(1)} %reshape.168.blend_ref, bf16[1024,1536]{1,0:T(8,128)(2,1)} %convolution_convert_fusion.q_ref.k_ref.v_ref, bf16[1024,1536]{1,0:T(8,128)(2,1)} %convolution_convert_fusion.q_ref.k_ref.v_ref, ...), custom_call_target="tpu_custom_call" | custom-call | flops 25165824000 | bytes 4194304 | tf_op jit(solution)/shard_map/pallas_call | solution.py:435
  67.4 28.3 %shard_map.238 = (bf16[1024,512]{1,0:T(8,128)(2,1)}, f32[1024,512]{1,0:T(8,128)}, f32[1024,512]{1,0:T(8,128)}, bf16[512,4608]{1,0:T(8,128)(2,1)}, f32[3,512]{1,0:T(4,128)}, /*index=5*/f32[1,2048]{1,0:T(1,128)}) custom-call(bf16[1024,512]{1,0:T(8,128)(2,1)} %bitcast.63, bf16[1024,512]{1,0:T(8,128)(2,1)} %copy-done.20, bf16[1024,512]{1,0:T(8,128)(2,1)} %bitcast.75, ...), custom_call_target="tpu_custom_call" | custom-call | flops 25769803776 | bytes 10485760 | tf_op jit(solution)/shard_map/pallas_call | solution.py:566
  95.7 13.0 %shard_map.242 = (bf16[1024,128]{1,0:T(8,128)(2,1)}, bf16[1024,128]{1,0:T(8,128)(2,1)}, bf16[1024,128]{1,0:T(8,128)(2,1)}, bf16[64,128]{1,0:T(8,128)(2,1)}, bf16...) custom-call(s32[2]{0:T(128)} %copy-done.7, f32[3,512]{1,0:T(4,128)} %copy-done.4, ...), custom_call_target="tpu_custom_call" | custom-call | flops 12582912000 | bytes 2097152 | tf_op jit(solution)/shard_map/pallas_call | solution.py:459
  108.7 12.8 %shard_map.241 = (bf16[1024,128]{1,0:T(8,128)(2,1)}, bf16[1024,128]{1,0:T(8,128)(2,1)}, bf16[1024,128]{1,0:T(8,128)(2,1)}, bf16[64,128]{1,0:T(8,128)(2,1)}, bf16...) custom-call(s32[2]{0:T(128)} %copy-done.7, f32[3,512]{1,0:T(4,128)} %copy-done.4, ...), custom_call_target="tpu_custom_call" | custom-call | flops 12582912000 | bytes 2097152 | tf_op jit(solution)/shard_map/pallas_call | solution.py:459
  121.5 12.8 %shard_map.240 = (bf16[1024,128]{1,0:T(8,128)(2,1)}, bf16[1024,128]{1,0:T(8,128)(2,1)}, bf16[1024,128]{1,0:T(8,128)(2,1)}, bf16[64,128]{1,0:T(8,128)(2,1)}, bf16...) custom-call(s32[2]{0:T(128)} %copy-done.7, f32[3,512]{1,0:T(4,128)} %copy-done.4, ...), custom_call_target="tpu_custom_call" | custom-call | flops 12582912000 | bytes 2097152 | tf_op jit(solution)/shard_map/pallas_call | solution.py:459
  134.4 12.9 %shard_map.239 = (bf16[1024,128]{1,0:T(8,128)(2,1)}, bf16[1024,128]{1,0:T(8,128)(2,1)}, bf16[1024,128]{1,0:T(8,128)(2,1)}, bf16[64,128]{1,0:T(8,128)(2,1)}, bf16...) custom-call(s32[2]{0:T(128)} %copy-done.7, f32[3,512]{1,0:T(4,128)} %copy-done.4, ...), custom_call_target="tpu_custom_call" | custom-call | flops 12582912000 | bytes 2097152 | tf_op jit(solution)/shard_map/pallas_call | solution.py:459
  151.0 8.5 %shard_map.243 = (bf16[1024,512]{1,0:T(8,128)(2,1)}, bf16[512,1792]{1,0:T(8,128)(2,1)}) custom-call(bf16[1024,512]{1,0:T(8,128)(2,1)S(1)} %bitcast.64, f32[1024,512]{1,0:T(8,128)} %get-tuple-element.45.first_ref, bf16[512,1536]{1,0:T(8,128)(2,1)} %w_ref.1, f32[1,512]{1,0:T(1,128)S(1)} %bitcast.66, f32[1,512]{1,0:T(1,128)S(1)} %bitcast.65, ...), custom_call_target="tpu_custom_call" | custom-call | flops 6442450944 | bytes 10485760 | tf_op jit(solution)/shard_map/pallas_call | solution.py:631
  160.9 3.4 %dynamic-slice_bitcast_fusion = bf16[16,16,4608]{2,1,0:T(8,128)(2,1)} fusion(bf16[2,16,16,4608]{3,2,1,0:T(8,128)(2,1)} %bitcast.69, s32[]{:T(128)S(6)} %select_n.117), kind=kLoop, calls=%fused_computation.5 | loop fusion | bytes 4718596 | tf_op jit(solution)/shard_map/jit(dynamic_index_in_dim)/squeeze | solution.py:699
  170.7 6.0 %all-to-all-start.2 = ((bf16[8,128,512]{2,1,0:T(8,128)(2,1)}), bf16[8,128,512]{2,1,0:T(8,128)(2,1)}, u32[]{:S(2)}, u32[]{:S(2)}) async-start(bf16[8,128,512]{2,1,0:T(8,128)(2,1)} %bitcast.74), calls=%async_computation.2 | async-start | bytes 2097152 | tf_op jit(solution)/shard_map/all_to_all | solution.py:653
  176.6 8.7 %collective-permute-done.1 = bf16[4,16,1792]{2,1,0:T(8,128)(2,1)S(1)} collective-permute-done((bf16[4,16,1792]{2,1,0:T(8,128)(2,1)}, bf16[4,16,1792]{2,1,0:T(8,128)(2,1)S(1)}, u32[]{:S(2)}, u32[]{:S(2)}) %collective-permute-start.1) | collective-permute-done | bytes 229408 | tf_op jit(solution)/shard_map/ppermute | solution.py:693
  188.8 2.3 collective-permute-start.6
  191.2 2.4 fusion
  193.7 2.6 collective-permute-start.15
  197.9 2.5 collective-permute-done.6
  200.4 6.6 %collective-permute-done.5 = bf16[1,16,1792]{2,1,0:T(8,128)(2,1)S(1)} collective-permute-done((bf16[1,16,1792]{2,1,0:T(8,128)(2,1)S(1)}, bf16[1,16,1792]{2,1,0:T(8,128)(2,1)S(1)}, u32[]{:S(2)}, u32[]{:S(2)}) %collective-permute-start.5) | collective-permute-done | bytes 57376 | tf_op jit(solution)/shard_map/ppermute | solution.py:693
  208.6 12.8 %collective-permute-done.15 = bf16[4,16,4608]{2,1,0:T(8,128)(2,1)S(1)} collective-permute-done((bf16[4,16,4608]{2,1,0:T(8,128)(2,1)S(1)}, bf16[4,16,4608]{2,1,0:T(8,128)(2,1)S(1)}, u32[]{:S(2)}, u32[]{:S(2)}) %collective-permute-start.15) | collective-permute-done | bytes 589856 | tf_op jit(solution)/shard_map/ppermute | solution.py:693
  221.4 2.9 collective-permute-start.9
  228.9 3.4 %collective-permute-start.12 = (bf16[4,16,1792]{2,1,0:T(8,128)(2,1)}, bf16[4,16,1792]{2,1,0:T(8,128)(2,1)}, u32[]{:S(2)}, u32[]{:S(2)}) collective-permute-start(bf16[4,16,1792]{2,1,0:T(8,128)(2,1)} %pad_maximum_fusion.3), channel_id=1, source_target_pairs={{0,6},{1,7},{2,4},{3,5},{4,2},{5,3},{6,0},{7,1},{8,14},{9,15},{10,... | collective-permute-start | bytes 688136 | tf_op jit(solution)/shard_map/ppermute | solution.py:693
  234.2 6.4 %collective-permute-done.19 = bf16[1,16,4608]{2,1,0:T(8,128)(2,1)S(1)} collective-permute-done((bf16[1,16,4608]{2,1,0:T(8,128)(2,1)S(1)}, bf16[1,16,4608]{2,1,0:T(8,128)(2,1)S(1)}, u32[]{:S(2)}, u32[]{:S(2)}) %collective-permute-start.19) | collective-permute-done | bytes 147488 | tf_op jit(solution)/shard_map/ppermute | solution.py:693
  242.3 2.8 collective-permute-start.21
  245.1 4.2 %collective-permute-done.23 = bf16[1,16,4608]{2,1,0:T(8,128)(2,1)S(1)} collective-permute-done((bf16[1,16,4608]{2,1,0:T(8,128)(2,1)S(1)}, bf16[1,16,4608]{2,1,0:T(8,128)(2,1)S(1)}, u32[]{:S(2)}, u32[]{:S(2)}) %collective-permute-start.23) | collective-permute-done | bytes 147488 | tf_op jit(solution)/shard_map/ppermute | solution.py:693
  257.1 13.2 %collective-permute-done.24 = bf16[4,16,4608]{2,1,0:T(8,128)(2,1)S(1)} collective-permute-done((bf16[4,16,4608]{2,1,0:T(8,128)(2,1)S(1)}, bf16[4,16,4608]{2,1,0:T(8,128)(2,1)S(1)}, u32[]{:S(2)}, u32[]{:S(2)}) %collective-permute-start.24) | collective-permute-done | bytes 589856 | tf_op jit(solution)/shard_map/ppermute | solution.py:693
  272.1 13.3 %collective-permute-done.26 = bf16[4,16,4608]{2,1,0:T(8,128)(2,1)S(1)} collective-permute-done((bf16[4,16,4608]{2,1,0:T(8,128)(2,1)S(1)}, bf16[4,16,4608]{2,1,0:T(8,128)(2,1)S(1)}, u32[]{:S(2)}, u32[]{:S(2)}) %collective-permute-start.26) | collective-permute-done | bytes 589856 | tf_op jit(solution)/shard_map/ppermute | solution.py:693
  285.6 4.3 %all-to-all-start.3 = ((bf16[8,128,512]{2,1,0:T(8,128)(2,1)}), bf16[8,128,512]{2,1,0:T(8,128)(2,1)}, u32[]{:S(2)}, u32[]{:S(2)}) async-start(bf16[8,128,512]{2,1,0:T(8,128)(2,1)} %bitcast.12), calls=%async_computation.3 | async-start | bytes 2097152 | tf_op jit(solution)/shard_map/all_to_all | solution.py:653
  293.3 23.2 %all-to-all-done.3 = bf16[8,128,512]{2,1,0:T(8,128)(2,1)} async-done(((bf16[8,128,512]{2,1,0:T(8,128)(2,1)}), bf16[8,128,512]{2,1,0:T(8,128)(2,1)}, u32[]{:S(2)}, u32[]{:S(2)}) %all-to-all-start.3) | async-done | bytes 1048608 | tf_op jit(solution)/shard_map/all_to_all | solution.py:653
  316.5 3.5 %shard_map.244 = (f32[512,1536]{1,0:T(8,128)}, f32[512,128]{1,0:T(8,128)S(1)}) custom-call(s32[32]{0:T(128)S(1)} %fusion.16.order_ref, bf16[16,16,1792]{2,1,0:T(8,128)(2,1)S(1)} %constant_dynamic-update-slice_fusion.own_ref, bf16[16,16,1792]{2,1,0:T(8,128)(2,1)} %collective-permute-done.13.other_ref), custom_call_target="tpu_custom_call" | custom-call | bytes 3670016 | tf_op jit(solution)/shard_map/pallas_call | solution.py:771
  322.0 6.4 %shard_map.245 = (f32[512,2048]{1,0:T(8,128)}, f32[512,512]{1,0:T(8,128)}, f32[2048,512]{1,0:T(8,128)}) custom-call(s32[32]{0:T(128)S(1)} %fusion.16.order_ref, bf16[16,16,4608]{2,1,0:T(8,128)(2,1)S(1)} %constant_dynamic-update-slice_fusion.7.own_ref, bf16[16,16,4608]{2,1,0:T(8,128)(2,1)} %collective-permute-done.27.other_ref), custom_call_target="tpu_custom_call" | custom-call | bytes 9437184 | tf_op jit(solution)/shard_map/pallas_call | solution.py:771
  328.4 2.3 copy.41
  (152 shorter events, 49.3 us)
Async XLA Ops:
  0.6 33.1 %all-to-all-start = ((bf16[8,128,512]{2,1,0:T(8,128)(2,1)}), bf16[8,128,512]{2,1,0:T(8,128)(2,1)S(1)}, u32[]{:S(2)}, u32[]{:S(2)}) async-start(bf16[8,128,512]{2,1,0:T(8,128)(2,1)} %param.14), calls=%async_computation | async-start | bytes 2097152 | tf_op jit(solution)/shard_map/all_to_all | solution.py:653
  33.7 32.7 %all-to-all-start.1 = ((bf16[8,128,512]{2,1,0:T(8,128)(2,1)}), bf16[8,128,512]{2,1,0:T(8,128)(2,1)S(1)}, u32[]{:S(2)}, u32[]{:S(2)}) async-start(bf16[8,128,512]{2,1,0:T(8,128)(2,1)} %param.15), calls=%async_computation.1 | async-start | bytes 2097152 | tf_op jit(solution)/shard_map/all_to_all | solution.py:653
  160.7 3.9 %collective-permute-start = (bf16[16,16,1792]{2,1,0:T(8,128)(2,1)S(1)}, bf16[16,16,1792]{2,1,0:T(8,128)(2,1)}, u32[]{:S(2)}, u32[]{:S(2)}) collective-permute-start(bf16[16,16,1792]{2,1,0:T(8,128)(2,1)S(1)} %dynamic-slice_bitcast_fusion.1), channel_id=1, source_target_pairs={{0,1},{1,0},{2,3},{3,2},{4,5},{5,4},{6,7},{7,6},{8,9},{9,8},{10,11... | collective-permute-start | bytes 2752520 | tf_op jit(solution)/shard_map/ppermute | solution.py:693
  164.2 26.9 %collective-permute-start.14 = (bf16[16,16,4608]{2,1,0:T(8,128)(2,1)}, bf16[16,16,4608]{2,1,0:T(8,128)(2,1)S(1)}, u32[]{:S(2)}, u32[]{:S(2)}) collective-permute-start(bf16[16,16,4608]{2,1,0:T(8,128)(2,1)} %dynamic-slice_bitcast_fusion), channel_id=1, source_target_pairs={{0,1},{1,0},{2,3},{3,2},{4,5},{5,4},{6,7},{7,6},{8,9},{9,8},{10,11... | collective-permute-start | bytes 7077896 | tf_op jit(solution)/shard_map/ppermute | solution.py:693
  167.1 18.2 %collective-permute-start.1 = (bf16[4,16,1792]{2,1,0:T(8,128)(2,1)}, bf16[4,16,1792]{2,1,0:T(8,128)(2,1)S(1)}, u32[]{:S(2)}, u32[]{:S(2)}) collective-permute-start(bf16[4,16,1792]{2,1,0:T(8,128)(2,1)} %get-tuple-element.80), channel_id=1, source_target_pairs={{0,4},{1,5},{2,6},{3,7},{4,0},{5,1},{6,2},{7,3},{8,12},{9,13},{10,... | collective-permute-start | bytes 688136 | tf_op jit(solution)/shard_map/ppermute | solution.py:693
  169.2 16.2 %collective-permute-start.3 = (bf16[4,16,1792]{2,1,0:T(8,128)(2,1)}, bf16[4,16,1792]{2,1,0:T(8,128)(2,1)}, u32[]{:S(2)}, u32[]{:S(2)}) collective-permute-start(bf16[4,16,1792]{2,1,0:T(8,128)(2,1)} %get-tuple-element.81), channel_id=1, source_target_pairs={{0,6},{1,7},{2,4},{3,5},{4,2},{5,3},{6,0},{7,1},{8,14},{9,15},{10,... | collective-permute-start | bytes 688136 | tf_op jit(solution)/shard_map/ppermute | solution.py:693
  170.1 15.2 %collective-permute-start.2 = (bf16[4,16,1792]{2,1,0:T(8,128)(2,1)}, bf16[4,16,1792]{2,1,0:T(8,128)(2,1)}, u32[]{:S(2)}, u32[]{:S(2)}) collective-permute-start(bf16[4,16,1792]{2,1,0:T(8,128)(2,1)} %get-tuple-element.82), channel_id=1, source_target_pairs={{0,2},{1,3},{2,0},{3,1},{4,6},{5,7},{6,4},{7,5},{8,10},{9,11},{10,... | collective-permute-start | bytes 688136 | tf_op jit(solution)/shard_map/ppermute | solution.py:693
  170.7 114.9 %all-to-all-start.2 = ((bf16[8,128,512]{2,1,0:T(8,128)(2,1)}), bf16[8,128,512]{2,1,0:T(8,128)(2,1)}, u32[]{:S(2)}, u32[]{:S(2)}) async-start(bf16[8,128,512]{2,1,0:T(8,128)(2,1)} %bitcast.74), calls=%async_computation.2 | async-start | bytes 2097152 | tf_op jit(solution)/shard_map/all_to_all | solution.py:653
  186.6 10.7 %collective-permute-start.4 = (bf16[1,16,1792]{2,1,0:T(8,128)(2,1)S(1)}, bf16[1,16,1792]{2,1,0:T(8,128)(2,1)S(1)}, u32[]{:S(2)}, u32[]{:S(2)}) collective-permute-start(bf16[1,16,1792]{2,1,0:T(8,128)(2,1)S(1)} %get-tuple-element.93), channel_id=1, source_target_pairs={{0,8},{1,9},{2,10},{3,11},{4,12},{5,13},{6,14},{7,15},{8,0},{9,1},... | collective-permute-start | bytes 172040 | tf_op jit(solution)/shard_map/ppermute | solution.py:693
  188.8 11.6 %collective-permute-start.6 = (bf16[1,16,1792]{2,1,0:T(8,128)(2,1)S(1)}, bf16[1,16,1792]{2,1,0:T(8,128)(2,1)S(1)}, u32[]{:S(2)}, u32[]{:S(2)}) collective-permute-start(bf16[1,16,1792]{2,1,0:T(8,128)(2,1)S(1)} %get-tuple-element.94), channel_id=1, source_target_pairs={{0,24},{1,25},{2,26},{3,27},{4,28},{5,29},{6,30},{7,31},{8,16},{9,... | collective-permute-start | bytes 172040 | tf_op jit(solution)/shard_map/ppermute | solution.py:693
  191.1 15.8 %collective-permute-start.5 = (bf16[1,16,1792]{2,1,0:T(8,128)(2,1)S(1)}, bf16[1,16,1792]{2,1,0:T(8,128)(2,1)S(1)}, u32[]{:S(2)}, u32[]{:S(2)}) collective-permute-start(bf16[1,16,1792]{2,1,0:T(8,128)(2,1)S(1)} %get-tuple-element.95), channel_id=1, source_target_pairs={{0,16},{1,17},{2,18},{3,19},{4,20},{5,21},{6,22},{7,23},{8,24},{9,... | collective-permute-start | bytes 172040 | tf_op jit(solution)/shard_map/ppermute | solution.py:693
  193.7 27.7 %collective-permute-start.15 = (bf16[4,16,4608]{2,1,0:T(8,128)(2,1)S(1)}, bf16[4,16,4608]{2,1,0:T(8,128)(2,1)S(1)}, u32[]{:S(2)}, u32[]{:S(2)}) collective-permute-start(bf16[4,16,4608]{2,1,0:T(8,128)(2,1)S(1)} %get-tuple-element.75), channel_id=1, source_target_pairs={{0,4},{1,5},{2,6},{3,7},{4,0},{5,1},{6,2},{7,3},{8,12},{9,13},{10,... | collective-permute-start | bytes 1769480 | tf_op jit(solution)/shard_map/ppermute | solution.py:693
  196.3 27.9 %collective-permute-start.17 = (bf16[4,16,4608]{2,1,0:T(8,128)(2,1)S(1)}, bf16[4,16,4608]{2,1,0:T(8,128)(2,1)S(1)}, u32[]{:S(2)}, u32[]{:S(2)}) collective-permute-start(bf16[4,16,4608]{2,1,0:T(8,128)(2,1)S(1)} %get-tuple-element.76), channel_id=1, source_target_pairs={{0,6},{1,7},{2,4},{3,5},{4,2},{5,3},{6,0},{7,1},{8,14},{9,15},{10,... | collective-permute-start | bytes 1769480 | tf_op jit(solution)/shard_map/ppermute | solution.py:693
  197.3 26.9 %collective-permute-start.16 = (bf16[4,16,4608]{2,1,0:T(8,128)(2,1)S(1)}, bf16[4,16,4608]{2,1,0:T(8,128)(2,1)S(1)}, u32[]{:S(2)}, u32[]{:S(2)}) collective-permute-start(bf16[4,16,4608]{2,1,0:T(8,128)(2,1)S(1)} %get-tuple-element.77), channel_id=1, source_target_pairs={{0,2},{1,3},{2,0},{3,1},{4,6},{5,7},{6,4},{7,5},{8,10},{9,11},{10,... | collective-permute-start | bytes 1769480 | tf_op jit(solution)/shard_map/ppermute | solution.py:693
  207.0 20.0 %collective-permute-start.8 = (bf16[1,16,1792]{2,1,0:T(8,128)(2,1)S(1)}, bf16[1,16,1792]{2,1,0:T(8,128)(2,1)S(1)}, u32[]{:S(2)}, u32[]{:S(2)}) collective-permute-start(bf16[1,16,1792]{2,1,0:T(8,128)(2,1)S(1)} %get-tuple-element.98), channel_id=1, source_target_pairs={{0,16},{1,17},{2,18},{3,19},{4,20},{5,21},{6,22},{7,23},{8,24},{9,... | collective-permute-start | bytes 172040 | tf_op jit(solution)/shard_map/ppermute | solution.py:693
  207.1 21.1 %collective-permute-start.7 = (bf16[1,16,1792]{2,1,0:T(8,128)(2,1)S(1)}, bf16[1,16,1792]{2,1,0:T(8,128)(2,1)S(1)}, u32[]{:S(2)}, u32[]{:S(2)}) collective-permute-start(bf16[1,16,1792]{2,1,0:T(8,128)(2,1)S(1)} %get-tuple-element.98), channel_id=1, source_target_pairs={{0,8},{1,9},{2,10},{3,11},{4,12},{5,13},{6,14},{7,15},{8,0},{9,1},... | collective-permute-start | bytes 172040 | tf_op jit(solution)/shard_map/ppermute | solution.py:693
  221.4 6.8 %collective-permute-start.9 = (bf16[1,16,1792]{2,1,0:T(8,128)(2,1)S(1)}, bf16[1,16,1792]{2,1,0:T(8,128)(2,1)S(1)}, u32[]{:S(2)}, u32[]{:S(2)}) collective-permute-start(bf16[1,16,1792]{2,1,0:T(8,128)(2,1)S(1)} %get-tuple-element.98), channel_id=1, source_target_pairs={{0,24},{1,25},{2,26},{3,27},{4,28},{5,29},{6,30},{7,31},{8,16},{9,... | collective-permute-start | bytes 172040 | tf_op jit(solution)/shard_map/ppermute | solution.py:693
  224.6 8.2 %collective-permute-start.18 = (bf16[1,16,4608]{2,1,0:T(8,128)(2,1)S(1)}, bf16[1,16,4608]{2,1,0:T(8,128)(2,1)S(1)}, u32[]{:S(2)}, u32[]{:S(2)}) collective-permute-start(bf16[1,16,4608]{2,1,0:T(8,128)(2,1)S(1)} %get-tuple-element.83), channel_id=1, source_target_pairs={{0,8},{1,9},{2,10},{3,11},{4,12},{5,13},{6,14},{7,15},{8,0},{9,1},... | collective-permute-start | bytes 442376 | tf_op jit(solution)/shard_map/ppermute | solution.py:693
  225.8 8.4 %collective-permute-start.20 = (bf16[1,16,4608]{2,1,0:T(8,128)(2,1)S(1)}, bf16[1,16,4608]{2,1,0:T(8,128)(2,1)S(1)}, u32[]{:S(2)}, u32[]{:S(2)}) collective-permute-start(bf16[1,16,4608]{2,1,0:T(8,128)(2,1)S(1)} %get-tuple-element.84), channel_id=1, source_target_pairs={{0,24},{1,25},{2,26},{3,27},{4,28},{5,29},{6,30},{7,31},{8,16},{9,... | collective-permute-start | bytes 442376 | tf_op jit(solution)/shard_map/ppermute | solution.py:693
  227.0 13.5 %collective-permute-start.19 = (bf16[1,16,4608]{2,1,0:T(8,128)(2,1)S(1)}, bf16[1,16,4608]{2,1,0:T(8,128)(2,1)S(1)}, u32[]{:S(2)}, u32[]{:S(2)}) collective-permute-start(bf16[1,16,4608]{2,1,0:T(8,128)(2,1)S(1)} %get-tuple-element.85), channel_id=1, source_target_pairs={{0,16},{1,17},{2,18},{3,19},{4,20},{5,21},{6,22},{7,23},{8,24},{9,... | collective-permute-start | bytes 442376 | tf_op jit(solution)/shard_map/ppermute | solution.py:693
  228.9 62.9 %collective-permute-start.12 = (bf16[4,16,1792]{2,1,0:T(8,128)(2,1)}, bf16[4,16,1792]{2,1,0:T(8,128)(2,1)}, u32[]{:S(2)}, u32[]{:S(2)}) collective-permute-start(bf16[4,16,1792]{2,1,0:T(8,128)(2,1)} %pad_maximum_fusion.3), channel_id=1, source_target_pairs={{0,6},{1,7},{2,4},{3,5},{4,2},{5,3},{6,0},{7,1},{8,14},{9,15},{10,... | collective-permute-start | bytes 688136 | tf_op jit(solution)/shard_map/ppermute | solution.py:693
  232.3 58.5 %collective-permute-start.11 = (bf16[4,16,1792]{2,1,0:T(8,128)(2,1)}, bf16[4,16,1792]{2,1,0:T(8,128)(2,1)}, u32[]{:S(2)}, u32[]{:S(2)}) collective-permute-start(bf16[4,16,1792]{2,1,0:T(8,128)(2,1)} %pad_maximum_fusion.3), channel_id=1, source_target_pairs={{0,2},{1,3},{2,0},{3,1},{4,6},{5,7},{6,4},{7,5},{8,10},{9,11},{10,... | collective-permute-start | bytes 688136 | tf_op jit(solution)/shard_map/ppermute | solution.py:693
  240.6 8.7 %collective-permute-start.23 = (bf16[1,16,4608]{2,1,0:T(8,128)(2,1)S(1)}, bf16[1,16,4608]{2,1,0:T(8,128)(2,1)S(1)}, u32[]{:S(2)}, u32[]{:S(2)}) collective-permute-start(bf16[1,16,4608]{2,1,0:T(8,128)(2,1)S(1)} %get-tuple-element.74), channel_id=1, source_target_pairs={{0,24},{1,25},{2,26},{3,27},{4,28},{5,29},{6,30},{7,31},{8,16},{9,... | collective-permute-start | bytes 442376 | tf_op jit(solution)/shard_map/ppermute | solution.py:693
  242.3 11.4 %collective-permute-start.22 = (bf16[1,16,4608]{2,1,0:T(8,128)(2,1)S(1)}, bf16[1,16,4608]{2,1,0:T(8,128)(2,1)S(1)}, u32[]{:S(2)}, u32[]{:S(2)}) collective-permute-start(bf16[1,16,4608]{2,1,0:T(8,128)(2,1)S(1)} %get-tuple-element.74), channel_id=1, source_target_pairs={{0,16},{1,17},{2,18},{3,19},{4,20},{5,21},{6,22},{7,23},{8,24},{9,... | collective-permute-start | bytes 442376 | tf_op jit(solution)/shard_map/ppermute | solution.py:693
  242.3 11.4 %collective-permute-start.21 = (bf16[1,16,4608]{2,1,0:T(8,128)(2,1)S(1)}, bf16[1,16,4608]{2,1,0:T(8,128)(2,1)S(1)}, u32[]{:S(2)}, u32[]{:S(2)}) collective-permute-start(bf16[1,16,4608]{2,1,0:T(8,128)(2,1)S(1)} %get-tuple-element.74), channel_id=1, source_target_pairs={{0,8},{1,9},{2,10},{3,11},{4,12},{5,13},{6,14},{7,15},{8,0},{9,1},... | collective-permute-start | bytes 442376 | tf_op jit(solution)/shard_map/ppermute | solution.py:693
  249.3 40.5 %collective-permute-start.10 = (bf16[4,16,1792]{2,1,0:T(8,128)(2,1)}, bf16[4,16,1792]{2,1,0:T(8,128)(2,1)}, u32[]{:S(2)}, u32[]{:S(2)}) collective-permute-start(bf16[4,16,1792]{2,1,0:T(8,128)(2,1)} %pad_maximum_fusion.3), channel_id=1, source_target_pairs={{0,4},{1,5},{2,6},{3,7},{4,0},{5,1},{6,2},{7,3},{8,12},{9,13},{10,... | collective-permute-start | bytes 688136 | tf_op jit(solution)/shard_map/ppermute | solution.py:693
  253.8 18.3 %collective-permute-start.25 = (bf16[4,16,4608]{2,1,0:T(8,128)(2,1)S(1)}, bf16[4,16,4608]{2,1,0:T(8,128)(2,1)S(1)}, u32[]{:S(2)}, u32[]{:S(2)}) collective-permute-start(bf16[4,16,4608]{2,1,0:T(8,128)(2,1)S(1)} %pad_maximum_fusion.1), channel_id=1, source_target_pairs={{0,2},{1,3},{2,0},{3,1},{4,6},{5,7},{6,4},{7,5},{8,10},{9,11},{10,... | collective-permute-start | bytes 1769480 | tf_op jit(solution)/shard_map/ppermute | solution.py:693
  255.2 15.1 %collective-permute-start.24 = (bf16[4,16,4608]{2,1,0:T(8,128)(2,1)S(1)}, bf16[4,16,4608]{2,1,0:T(8,128)(2,1)S(1)}, u32[]{:S(2)}, u32[]{:S(2)}) collective-permute-start(bf16[4,16,4608]{2,1,0:T(8,128)(2,1)S(1)} %pad_maximum_fusion.1), channel_id=1, source_target_pairs={{0,4},{1,5},{2,6},{3,7},{4,0},{5,1},{6,2},{7,3},{8,12},{9,13},{10,... | collective-permute-start | bytes 1769480 | tf_op jit(solution)/shard_map/ppermute | solution.py:693
  270.3 15.1 %collective-permute-start.26 = (bf16[4,16,4608]{2,1,0:T(8,128)(2,1)S(1)}, bf16[4,16,4608]{2,1,0:T(8,128)(2,1)S(1)}, u32[]{:S(2)}, u32[]{:S(2)}) collective-permute-start(bf16[4,16,4608]{2,1,0:T(8,128)(2,1)S(1)} %pad_maximum_fusion.1), channel_id=1, source_target_pairs={{0,6},{1,7},{2,4},{3,5},{4,2},{5,3},{6,0},{7,1},{8,14},{9,15},{10,... | collective-permute-start | bytes 1769480 | tf_op jit(solution)/shard_map/ppermute | solution.py:693
  285.5 36.5 %collective-permute-start.27 = (bf16[16,16,4608]{2,1,0:T(8,128)(2,1)S(1)}, bf16[16,16,4608]{2,1,0:T(8,128)(2,1)}, u32[]{:S(2)}, u32[]{:S(2)}) collective-permute-start(bf16[16,16,4608]{2,1,0:T(8,128)(2,1)S(1)} %constant_dynamic-update-slice_fusion.7.own_ref), channel_id=1, source_target_pairs={{0,1},{1,0},{2,3},{3,2},{4,5},{5,4},{6,7},{7,6},{8,9},{9,8},{10,11... | collective-permute-start | bytes 7077896 | tf_op jit(solution)/shard_map/ppermute | solution.py:693
  285.6 31.0 %all-to-all-start.3 = ((bf16[8,128,512]{2,1,0:T(8,128)(2,1)}), bf16[8,128,512]{2,1,0:T(8,128)(2,1)}, u32[]{:S(2)}, u32[]{:S(2)}) async-start(bf16[8,128,512]{2,1,0:T(8,128)(2,1)} %bitcast.12), calls=%async_computation.3 | async-start | bytes 2097152 | tf_op jit(solution)/shard_map/all_to_all | solution.py:653
  292.7 23.8 %collective-permute-start.13 = (bf16[16,16,1792]{2,1,0:T(8,128)(2,1)S(1)}, bf16[16,16,1792]{2,1,0:T(8,128)(2,1)}, u32[]{:S(2)}, u32[]{:S(2)}) collective-permute-start(bf16[16,16,1792]{2,1,0:T(8,128)(2,1)S(1)} %constant_dynamic-update-slice_fusion.own_ref), channel_id=1, source_target_pairs={{0,1},{1,0},{2,3},{3,2},{4,5},{5,4},{6,7},{7,6},{8,9},{9,8},{10,11... | collective-permute-start | bytes 2752520 | tf_op jit(solution)/shard_map/ppermute | solution.py:693
  (28 other events, 393.9 us)
where the time goes:
time: 334 us; the launch traced here: 333 us
  Pallas kernels  120 us (36%)
  waiting for transfers between devices  117 us (35%)
  starting transfers between devices  57.9 us (17%)
  local copies, waits for them, and re-layouts  21.7 us (6%)
  other arithmetic  9.14 us (3%)
  matrix products  4.98 us (1%)
    ppermute x28, waiting for transfers between devices, swap(): return lax.ppermute(value, ('seq', 'batch'), route)  71.3 us
    pallas_call x4, Pallas kernels, attend_back(): pl.pallas_call(functools.partial(attend_back_kernel, together), grid=(1,)...  51.5 us
    all_to_all x4, waiting for transfers between devices, to_sequences(): return lax.all_to_all(block, axis, 0, 0, axis_index_groups=groups)  46.1 us
    ppermute x28, starting transfers between devices, swap(): return lax.ppermute(value, ('seq', 'batch'), route)  36.8 us
    pallas_call x1, Pallas kernels, feed_forward(): pl.pallas_call(functools.partial(feed_kernel, pieces), out_shape=(jax.Sha...  28.3 us
    pallas_call x1, Pallas kernels, attend(): pl.pallas_call(attend_kernel, grid=(1,), out_shape=shapes, in_specs=ins +...  22.2 us
    all_to_all x4, starting transfers between devices, to_sequences(): return lax.all_to_all(block, axis, 0, 0, axis_index_groups=groups)  21.1 us
    unnamed x68, local copies, waits for them, and re-layouts  11.5 us
  transfers between devices with their start and end apart: 32, of which 12 were waited for; matrix products, arithmetic and copies ran while one was open for 7% of the time, Pallas kernels for 8%

commit v1 on v0

--- a/solution.py
+++ b/solution.py
@@ -653,6 +653,10 @@
     return lax.all_to_all(block, axis, 0, 0, axis_index_groups=groups)
 
 
+def after(value, *others):
+    return lax.optimization_barrier((value,) + others)[0]
+
+
 def from_parts(total, axis, parts, stride, forward):
     size = lax.axis_size(axis)
     low = total.astype(BF16)
@@ -713,13 +717,19 @@
         parts = [value] + [self.swap(value, level, k) for k in range(1, self.sizes[level])]
         return jnp.concatenate(parts, 0)
 
-    def reduce(self, value, fine=0):
-        value = value.reshape(self.pieces, value.shape[0] // self.pieces, value.shape[1])
-        for level in ("core", "near", "far"):
-            value = self.scatter(value, level, fine)
+    def to_pieces(self, value):
+        return value.reshape(self.pieces, value.shape[0] // self.pieces, value.shape[1])
+
+    def halves(self, value):
         for level in ("far", "near"):
             value = self.gather(value, level)
         return value, self.swap(value, "core", 1)
+
+    def reduce(self, value, fine=0):
+        value = self.to_pieces(value)
+        for level in ("core", "near", "far"):
+            value = self.scatter(value, level, fine)
+        return self.halves(value)
 
     def order(self):
         me = self.mine()
@@ -834,21 +844,29 @@
         in_weight, in_bias, down_weight, down_bias,
     )
     output = to_sequences(result.reshape(seqs, span, width), "seq", groups)
+    calls = 4
+
+    def back(meta, number, later):
+        return attend_back(meta, blend, qkv, halo, state, later, grad_o, calls, number)
+
+    if parts > 1:
+        total = jnp.concatenate([back(meta, number, later)[6] for number in range(calls)], 1)
+        later = from_parts(total, "seq", parts, seqs, False)
+    backs, turn = [], meta
     if by_ring:
-        feed_halves = ring.reduce(feed_grads)
-
-    calls = 4
-
-    def back(later):
-        return [
-            attend_back(meta, blend, qkv, halo, state, later, grad_o, calls, number)
-            for number in range(calls)
-        ]
-
-    if parts > 1:
-        total = jnp.concatenate([call[6] for call in back(later)], 1)
-        later = from_parts(total, "seq", parts, seqs, False)
-    backs = back(later)
+        held = ring.to_pieces(feed_grads)
+        rounds = {1: "core", 3: "near"}
+        for number in range(calls):
+            if number in rounds:
+                held = ring.scatter(held, rounds[number], 0)
+                turn = after(turn, held)
+            backs.append(back(turn, number, later))
+            turn = after(turn, backs[-1][5])
+        held = ring.scatter(held, "far", 0)
+        grad_first = after(grad_first, held, output)
+        feed_halves = ring.halves(held)
+    else:
+        backs = [back(meta, number, later) for number in range(calls)]
     grads = [[call[part] for call in backs] for part in range(3)]
     if parts > 1:
         homeward = [(i + seqs, i) for i in range(devices - seqs)]

time: 334 us -> 301 us (0.901)
  waiting for transfers between devices: 117 us -> 79 us
  local copies, waits for them, and re-layouts: 21.7 us -> 30.2 us
    all_to_all x4, waiting for transfers between devices: 46.1 us -> 22.9 us  [to_sequences(): return lax.all_to_all(block, axis, 0, 0, axis_index_groups=groups)]
    ppermute x28, waiting for transfers between devices: 71.3 us -> 56.1 us  [swap(): return lax.ppermute(value, ('seq', 'batch'), route)]
    unnamed x68 -> x74, local copies, waits for them, and re-layouts: 11.5 us -> 21.8 us
    ppermute x28, starting transfers between devices: 36.8 us -> 33 us  [swap(): return lax.ppermute(value, ('seq', 'batch'), route)]
  transfers between devices with their start and end apart: 32 -> 32, of which waited for: 12 -> 13; matrix products, arithmetic and copies ran while one was open for 7% -> 7% of each run, Pallas kernels for 8% -> 29%
where the time goes in v1:
time: 301 us; the launch traced here: 300 us
  Pallas kernels  120 us (40%)
  waiting for transfers between devices  79 us (26%)
  starting transfers between devices  55.9 us (19%)
  local copies, waits for them, and re-layouts  30.2 us (10%)
  other arithmetic  8.03 us (3%)
  matrix products  4.98 us (2%)
    ppermute x28, waiting for transfers between devices, swap(): return lax.ppermute(value, ('seq', 'batch'), route)  56.1 us
    pallas_call x4, Pallas kernels, attend_back(): pl.pallas_call(functools.partial(attend_back_kernel, together), grid=(1,)...  51.6 us
    ppermute x28, starting transfers between devices, swap(): return lax.ppermute(value, ('seq', 'batch'), route)  33 us
    pallas_call x1, Pallas kernels, feed_forward(): pl.pallas_call(functools.partial(feed_kernel, pieces), out_shape=(jax.Sha...  28.3 us
    all_to_all x4, waiting for transfers between devices, to_sequences(): return lax.all_to_all(block, axis, 0, 0, axis_index_groups=groups)  22.9 us
    all_to_all x4, starting transfers between devices, to_sequences(): return lax.all_to_all(block, axis, 0, 0, axis_index_groups=groups)  22.9 us
    pallas_call x1, Pallas kernels, attend(): pl.pallas_call(attend_kernel, grid=(1,), out_shape=shapes, in_specs=ins +...  22.2 us
    unnamed x74, local copies, waits for them, and re-layouts  21.8 us
  transfers between devices with their start and end apart: 32, of which 13 were waited for; matrix products, arithmetic and copies ran while one was open for 7% of the time, Pallas kernels for 29%

profile of v1, /device:TPU:0, one launch (start us, length us, event | category | flops | bytes accessed | tf_op | source)
XLA Modules:
  0.0 299.6 jit_solution(10968640240295568978)
XLA Ops:
  0.6 7.3 %all-to-all-start = ((bf16[8,128,512]{2,1,0:T(8,128)(2,1)}), bf16[8,128,512]{2,1,0:T(8,128)(2,1)S(1)}, u32[]{:S(2)}, u32[]{:S(2)}) async-start(bf16[8,128,512]{2,1,0:T(8,128)(2,1)} %param.14), calls=%async_computation | async-start | bytes 2097152 | tf_op jit(solution)/shard_map/all_to_all | solution.py:653
  10.8 22.9 %all-to-all-done = bf16[8,128,512]{2,1,0:T(8,128)(2,1)S(1)} async-done(((bf16[8,128,512]{2,1,0:T(8,128)(2,1)}), bf16[8,128,512]{2,1,0:T(8,128)(2,1)S(1)}, u32[]{:S(2)}, u32[]{:S(2)}) %all-to-all-start) | async-done | bytes 1048608 | tf_op jit(solution)/shard_map/all_to_all | solution.py:653
  33.7 3.6 %all-to-all-start.1 = ((bf16[8,128,512]{2,1,0:T(8,128)(2,1)}), bf16[8,128,512]{2,1,0:T(8,128)(2,1)S(1)}, u32[]{:S(2)}, u32[]{:S(2)}) async-start(bf16[8,128,512]{2,1,0:T(8,128)(2,1)} %param.15), calls=%async_computation.1 | async-start | bytes 2097152 | tf_op jit(solution)/shard_map/all_to_all | solution.py:653
  38.1 5.0 %convolution_convert_fusion.q_ref.k_ref.v_ref = bf16[1024,1536]{1,0:T(8,128)(2,1)} fusion(bf16[512,1536]{1,0:T(8,128)(2,1)} %w_ref.1, bf16[1024,512]{1,0:T(8,128)(2,1)S(1)} %bitcast.62, f32[512]{0:T(512)S(1)} %copy-done.6, f32[512]{0:T(512)S(1)} %copy-done.7, f32[1024]{0:T(1024)S(1)} %rsqrt_bitcast_fusion, f32[1024]{0:T(1024)S(1)} %get-tuple-element.112), kind=kOutput, calls=%fused_computation.2 | convolution fusion | flops 1615331328 | bytes 5779456 | tf_op jit(solution)/shard_map/dot_general | solution.py:39
  43.2 22.2 %shard_map.237 = (bf16[1024,512]{1,0:T(8,128)(2,1)S(1)}, f32[2,4,128,256]{3,2,1,0:T(8,128)}) custom-call(s32[2]{0:T(128)S(1)} %pad_add_fusion.meta_ref, f32[3,512]{1,0:T(4,128)S(1)} %reshape.168.blend_ref, bf16[1024,1536]{1,0:T(8,128)(2,1)} %convolution_convert_fusion.q_ref.k_ref.v_ref, bf16[1024,1536]{1,0:T(8,128)(2,1)} %convolution_convert_fusion.q_ref.k_ref.v_ref, ...), custom_call_target="tpu_custom_call" | custom-call | flops 25165824000 | bytes 4194304 | tf_op jit(solution)/shard_map/pallas_call | solution.py:435
  67.4 28.3 %shard_map.238 = (bf16[1024,512]{1,0:T(8,128)(2,1)}, f32[1024,512]{1,0:T(8,128)}, f32[1024,512]{1,0:T(8,128)}, bf16[512,4608]{1,0:T(8,128)(2,1)}, f32[3,512]{1,0:T(4,128)}, /*index=5*/f32[1,2048]{1,0:T(1,128)}) custom-call(bf16[1024,512]{1,0:T(8,128)(2,1)} %bitcast.63, bf16[1024,512]{1,0:T(8,128)(2,1)} %copy-done.21, bf16[1024,512]{1,0:T(8,128)(2,1)} %bitcast.77, ...), custom_call_target="tpu_custom_call" | custom-call | flops 25769803776 | bytes 10485760 | tf_op jit(solution)/shard_map/pallas_call | solution.py:566
  95.7 3.2 %dynamic-slice_bitcast_fusion = bf16[16,16,4608]{2,1,0:T(8,128)(2,1)} fusion(bf16[2,16,16,4608]{3,2,1,0:T(8,128)(2,1)} %bitcast.70, s32[]{:T(128)S(6)} %select_n.110), kind=kLoop, calls=%fused_computation.5 | loop fusion | bytes 4718596 | tf_op jit(solution)/shard_map/jit(dynamic_index_in_dim)/squeeze | solution.py:703
  98.9 6.1 %all-to-all-start.2 = ((bf16[8,128,512]{2,1,0:T(8,128)(2,1)}), bf16[8,128,512]{2,1,0:T(8,128)(2,1)}, u32[]{:S(2)}, u32[]{:S(2)}) async-start(bf16[8,128,512]{2,1,0:T(8,128)(2,1)} %bitcast.9), calls=%async_computation.2 | async-start | bytes 2097152 | tf_op jit(solution)/shard_map/all_to_all | solution.py:653
  105.0 12.9 %shard_map.239 = (bf16[1024,128]{1,0:T(8,128)(2,1)}, bf16[1024,128]{1,0:T(8,128)(2,1)}, bf16[1024,128]{1,0:T(8,128)(2,1)}, bf16[64,128]{1,0:T(8,128)(2,1)}, bf16...) custom-call(s32[2]{0:T(128)} %copy-done.8, f32[3,512]{1,0:T(4,128)} %copy-done.5, ...), custom_call_target="tpu_custom_call" | custom-call | flops 12582912000 | bytes 2097152 | tf_op jit(solution)/shard_map/pallas_call | solution.py:459
  118.0 2.4 fusion
  120.6 3.0 collective-permute-start.3
  124.2 12.8 %shard_map.240 = (bf16[1024,128]{1,0:T(8,128)(2,1)}, bf16[1024,128]{1,0:T(8,128)(2,1)}, bf16[1024,128]{1,0:T(8,128)(2,1)}, bf16[64,128]{1,0:T(8,128)(2,1)}, bf16...) custom-call(s32[2]{0:T(128)} %copy-done.8, f32[3,512]{1,0:T(4,128)} %copy-done.5, ...), custom_call_target="tpu_custom_call" | custom-call | flops 12582912000 | bytes 2097152 | tf_op jit(solution)/shard_map/pallas_call | solution.py:459
  137.0 12.8 %shard_map.241 = (bf16[1024,128]{1,0:T(8,128)(2,1)}, bf16[1024,128]{1,0:T(8,128)(2,1)}, bf16[1024,128]{1,0:T(8,128)(2,1)}, bf16[64,128]{1,0:T(8,128)(2,1)}, bf16...) custom-call(s32[2]{0:T(128)} %copy-done.8, f32[3,512]{1,0:T(4,128)} %copy-done.5, ...), custom_call_target="tpu_custom_call" | custom-call | flops 12582912000 | bytes 2097152 | tf_op jit(solution)/shard_map/pallas_call | solution.py:459
  152.0 4.2 %collective-permute-start.6 = (bf16[1,16,4608]{2,1,0:T(8,128)(2,1)S(1)}, bf16[1,16,4608]{2,1,0:T(8,128)(2,1)S(1)}, u32[]{:S(2)}, u32[]{:S(2)}) collective-permute-start(bf16[1,16,4608]{2,1,0:T(8,128)(2,1)S(1)} %get-tuple-element.96), channel_id=1, source_target_pairs={{0,24},{1,25},{2,26},{3,27},{4,28},{5,29},{6,30},{7,31},{8,16},{9,... | collective-permute-start | bytes 442376 | tf_op jit(solution)/shard_map/ppermute | solution.py:697
  157.0 13.0 %shard_map.242 = (bf16[1024,128]{1,0:T(8,128)(2,1)}, bf16[1024,128]{1,0:T(8,128)(2,1)}, bf16[1024,128]{1,0:T(8,128)(2,1)}, bf16[64,128]{1,0:T(8,128)(2,1)}, bf16...) custom-call(s32[2]{0:T(128)} %copy-done.8, f32[3,512]{1,0:T(4,128)} %copy-done.5, ...), custom_call_target="tpu_custom_call" | custom-call | flops 12582912000 | bytes 2097152 | tf_op jit(solution)/shard_map/pallas_call | solution.py:459
  172.9 2.9 collective-permute-start.22
  187.3 8.2 %shard_map.243 = (bf16[1024,512]{1,0:T(8,128)(2,1)S(1)}, bf16[512,1792]{1,0:T(8,128)(2,1)}) custom-call(bf16[1024,512]{1,0:T(8,128)(2,1)S(1)} %bitcast.64, f32[1024,512]{1,0:T(8,128)} %get-tuple-element.53.first_ref, bf16[512,1536]{1,0:T(8,128)(2,1)} %w_ref.1, f32[1,512]{1,0:T(1,128)S(1)} %bitcast.67, f32[1,512]{1,0:T(1,128)S(1)} %bitcast.66, ...), custom_call_target="tpu_custom_call" | custom-call | flops 6442450944 | bytes 10485760 | tf_op jit(solution)/shard_map/pallas_call | solution.py:631
  196.5 5.9 %all-to-all-start.3 = ((bf16[8,128,512]{2,1,0:T(8,128)(2,1)}), bf16[8,128,512]{2,1,0:T(8,128)(2,1)}, u32[]{:S(2)}, u32[]{:S(2)}) async-start(bf16[8,128,512]{2,1,0:T(8,128)(2,1)} %bitcast.65), calls=%async_computation.3 | async-start | bytes 2097152 | tf_op jit(solution)/shard_map/all_to_all | solution.py:653
  212.1 2.9 collective-permute-start.10
  215.5 29.7 %collective-permute-done.24 = bf16[4,16,4608]{2,1,0:T(8,128)(2,1)S(1)} collective-permute-done((bf16[4,16,4608]{2,1,0:T(8,128)(2,1)S(1)}, bf16[4,16,4608]{2,1,0:T(8,128)(2,1)S(1)}, u32[]{:S(2)}, u32[]{:S(2)}) %collective-permute-start.24) | collective-permute-done | bytes 589856 | tf_op jit(solution)/shard_map/ppermute | solution.py:697
  246.6 5.7 %collective-permute-done.8 = bf16[4,16,1792]{2,1,0:T(8,128)(2,1)S(1)} collective-permute-done((bf16[4,16,1792]{2,1,0:T(8,128)(2,1)S(1)}, bf16[4,16,1792]{2,1,0:T(8,128)(2,1)S(1)}, u32[]{:S(2)}, u32[]{:S(2)}) %collective-permute-start.8) | collective-permute-done | bytes 229408 | tf_op jit(solution)/shard_map/ppermute | solution.py:697
  252.5 4.0 %collective-permute-start.13 = (bf16[1,16,1792]{2,1,0:T(8,128)(2,1)S(1)}, bf16[1,16,1792]{2,1,0:T(8,128)(2,1)S(1)}, u32[]{:S(2)}, u32[]{:S(2)}) collective-permute-start(bf16[1,16,1792]{2,1,0:T(8,128)(2,1)S(1)} %get-tuple-element.106), channel_id=1, source_target_pairs={{0,24},{1,25},{2,26},{3,27},{4,28},{5,29},{6,30},{7,31},{8,16},{9,... | collective-permute-start | bytes 172040 | tf_op jit(solution)/shard_map/ppermute | solution.py:697
  258.8 2.8 collective-permute-done.12
  263.9 2.2 collective-permute-start.16
  267.1 2.9 collective-permute-done.16
  273.6 4.4 %collective-permute-done.17 = bf16[4,16,1792]{2,1,0:T(8,128)(2,1)S(1)} collective-permute-done((bf16[4,16,1792]{2,1,0:T(8,128)(2,1)S(1)}, bf16[4,16,1792]{2,1,0:T(8,128)(2,1)S(1)}, u32[]{:S(2)}, u32[]{:S(2)}) %collective-permute-start.17) | collective-permute-done | bytes 229408 | tf_op jit(solution)/shard_map/ppermute | solution.py:697
  278.1 2.4 collective-permute-done.19
  280.6 2.6 collective-permute-done.20.other_ref
  283.2 3.5 %shard_map.244 = (f32[512,1536]{1,0:T(8,128)}, f32[512,128]{1,0:T(8,128)S(1)}) custom-call(s32[32]{0:T(128)S(1)} %fusion.16.order_ref, bf16[16,16,1792]{2,1,0:T(8,128)(2,1)S(1)} %constant_dynamic-update-slice_fusion.own_ref, bf16[16,16,1792]{2,1,0:T(8,128)(2,1)} %collective-permute-done.20.other_ref), custom_call_target="tpu_custom_call" | custom-call | bytes 3670016 | tf_op jit(solution)/shard_map/pallas_call | solution.py:781
  288.6 6.4 %shard_map.245 = (f32[512,2048]{1,0:T(8,128)}, f32[512,512]{1,0:T(8,128)}, f32[2048,512]{1,0:T(8,128)}) custom-call(s32[32]{0:T(128)S(1)} %fusion.16.order_ref, bf16[16,16,4608]{2,1,0:T(8,128)(2,1)S(1)} %constant_dynamic-update-slice_fusion.7.own_ref, bf16[16,16,4608]{2,1,0:T(8,128)(2,1)} %collective-permute-done.27.other_ref), custom_call_target="tpu_custom_call" | custom-call | bytes 9437184 | tf_op jit(solution)/shard_map/pallas_call | solution.py:781
  295.0 2.3 copy.41
  297.3 2.3 copy.42
  (159 shorter events, 47.4 us)
Async XLA Ops:
  0.6 33.1 %all-to-all-start = ((bf16[8,128,512]{2,1,0:T(8,128)(2,1)}), bf16[8,128,512]{2,1,0:T(8,128)(2,1)S(1)}, u32[]{:S(2)}, u32[]{:S(2)}) async-start(bf16[8,128,512]{2,1,0:T(8,128)(2,1)} %param.14), calls=%async_computation | async-start | bytes 2097152 | tf_op jit(solution)/shard_map/all_to_all | solution.py:653
  33.7 32.7 %all-to-all-start.1 = ((bf16[8,128,512]{2,1,0:T(8,128)(2,1)}), bf16[8,128,512]{2,1,0:T(8,128)(2,1)S(1)}, u32[]{:S(2)}, u32[]{:S(2)}) async-start(bf16[8,128,512]{2,1,0:T(8,128)(2,1)} %param.15), calls=%async_computation.1 | async-start | bytes 2097152 | tf_op jit(solution)/shard_map/all_to_all | solution.py:653
  98.9 19.1 %collective-permute-start = (bf16[16,16,4608]{2,1,0:T(8,128)(2,1)}, bf16[16,16,4608]{2,1,0:T(8,128)(2,1)}, u32[]{:S(2)}, u32[]{:S(2)}) collective-permute-start(bf16[16,16,4608]{2,1,0:T(8,128)(2,1)} %dynamic-slice_bitcast_fusion), channel_id=1, source_target_pairs={{0,1},{1,0},{2,3},{3,2},{4,5},{5,4},{6,7},{7,6},{8,9},{9,8},{10,11... | collective-permute-start | bytes 7077896 | tf_op jit(solution)/shard_map/ppermute | solution.py:697
  98.9 77.0 %all-to-all-start.2 = ((bf16[8,128,512]{2,1,0:T(8,128)(2,1)}), bf16[8,128,512]{2,1,0:T(8,128)(2,1)}, u32[]{:S(2)}, u32[]{:S(2)}) async-start(bf16[8,128,512]{2,1,0:T(8,128)(2,1)} %bitcast.9), calls=%async_computation.2 | async-start | bytes 2097152 | tf_op jit(solution)/shard_map/all_to_all | solution.py:653
  120.6 29.2 %collective-permute-start.3 = (bf16[4,16,4608]{2,1,0:T(8,128)(2,1)S(1)}, bf16[4,16,4608]{2,1,0:T(8,128)(2,1)S(1)}, u32[]{:S(2)}, u32[]{:S(2)}) collective-permute-start(bf16[4,16,4608]{2,1,0:T(8,128)(2,1)S(1)} %get-tuple-element.88), channel_id=1, source_target_pairs={{0,6},{1,7},{2,4},{3,5},{4,2},{5,3},{6,0},{7,1},{8,14},{9,15},{10,... | collective-permute-start | bytes 1769480 | tf_op jit(solution)/shard_map/ppermute | solution.py:697
  123.6 28.1 %collective-permute-start.2 = (bf16[4,16,4608]{2,1,0:T(8,128)(2,1)S(1)}, bf16[4,16,4608]{2,1,0:T(8,128)(2,1)S(1)}, u32[]{:S(2)}, u32[]{:S(2)}) collective-permute-start(bf16[4,16,4608]{2,1,0:T(8,128)(2,1)S(1)} %get-tuple-element.89), channel_id=1, source_target_pairs={{0,2},{1,3},{2,0},{3,1},{4,6},{5,7},{6,4},{7,5},{8,10},{9,11},{10,... | collective-permute-start | bytes 1769480 | tf_op jit(solution)/shard_map/ppermute | solution.py:697
  124.1 27.6 %collective-permute-start.1 = (bf16[4,16,4608]{2,1,0:T(8,128)(2,1)S(1)}, bf16[4,16,4608]{2,1,0:T(8,128)(2,1)S(1)}, u32[]{:S(2)}, u32[]{:S(2)}) collective-permute-start(bf16[4,16,4608]{2,1,0:T(8,128)(2,1)S(1)} %get-tuple-element.87), channel_id=1, source_target_pairs={{0,4},{1,5},{2,6},{3,7},{4,0},{5,1},{6,2},{7,3},{8,12},{9,13},{10,... | collective-permute-start | bytes 1769480 | tf_op jit(solution)/shard_map/ppermute | solution.py:697
  152.0 18.7 %collective-permute-start.6 = (bf16[1,16,4608]{2,1,0:T(8,128)(2,1)S(1)}, bf16[1,16,4608]{2,1,0:T(8,128)(2,1)S(1)}, u32[]{:S(2)}, u32[]{:S(2)}) collective-permute-start(bf16[1,16,4608]{2,1,0:T(8,128)(2,1)S(1)} %get-tuple-element.96), channel_id=1, source_target_pairs={{0,24},{1,25},{2,26},{3,27},{4,28},{5,29},{6,30},{7,31},{8,16},{9,... | collective-permute-start | bytes 442376 | tf_op jit(solution)/shard_map/ppermute | solution.py:697
  156.3 14.5 %collective-permute-start.5 = (bf16[1,16,4608]{2,1,0:T(8,128)(2,1)S(1)}, bf16[1,16,4608]{2,1,0:T(8,128)(2,1)S(1)}, u32[]{:S(2)}, u32[]{:S(2)}) collective-permute-start(bf16[1,16,4608]{2,1,0:T(8,128)(2,1)S(1)} %get-tuple-element.97), channel_id=1, source_target_pairs={{0,16},{1,17},{2,18},{3,19},{4,20},{5,21},{6,22},{7,23},{8,24},{9,... | collective-permute-start | bytes 442376 | tf_op jit(solution)/shard_map/ppermute | solution.py:697
  156.3 14.4 %collective-permute-start.4 = (bf16[1,16,4608]{2,1,0:T(8,128)(2,1)S(1)}, bf16[1,16,4608]{2,1,0:T(8,128)(2,1)S(1)}, u32[]{:S(2)}, u32[]{:S(2)}) collective-permute-start(bf16[1,16,4608]{2,1,0:T(8,128)(2,1)S(1)} %get-tuple-element.95), channel_id=1, source_target_pairs={{0,8},{1,9},{2,10},{3,11},{4,12},{5,13},{6,14},{7,15},{8,0},{9,1},... | collective-permute-start | bytes 442376 | tf_op jit(solution)/shard_map/ppermute | solution.py:697
  171.5 32.4 %collective-permute-start.21 = (bf16[1,16,4608]{2,1,0:T(8,128)(2,1)}, bf16[1,16,4608]{2,1,0:T(8,128)(2,1)}, u32[]{:S(2)}, u32[]{:S(2)}) collective-permute-start(bf16[1,16,4608]{2,1,0:T(8,128)(2,1)} %get-tuple-element.86), channel_id=1, source_target_pairs={{0,8},{1,9},{2,10},{3,11},{4,12},{5,13},{6,14},{7,15},{8,0},{9,1},... | collective-permute-start | bytes 442376 | tf_op jit(solution)/shard_map/ppermute | solution.py:697
  172.9 31.0 %collective-permute-start.22 = (bf16[1,16,4608]{2,1,0:T(8,128)(2,1)}, bf16[1,16,4608]{2,1,0:T(8,128)(2,1)}, u32[]{:S(2)}, u32[]{:S(2)}) collective-permute-start(bf16[1,16,4608]{2,1,0:T(8,128)(2,1)} %get-tuple-element.86), channel_id=1, source_target_pairs={{0,16},{1,17},{2,18},{3,19},{4,20},{5,21},{6,22},{7,23},{8,24},{9,... | collective-permute-start | bytes 442376 | tf_op jit(solution)/shard_map/ppermute | solution.py:697
  175.8 28.1 %collective-permute-start.23 = (bf16[1,16,4608]{2,1,0:T(8,128)(2,1)}, bf16[1,16,4608]{2,1,0:T(8,128)(2,1)}, u32[]{:S(2)}, u32[]{:S(2)}) collective-permute-start(bf16[1,16,4608]{2,1,0:T(8,128)(2,1)} %get-tuple-element.86), channel_id=1, source_target_pairs={{0,24},{1,25},{2,26},{3,27},{4,28},{5,29},{6,30},{7,31},{8,16},{9,... | collective-permute-start | bytes 442376 | tf_op jit(solution)/shard_map/ppermute | solution.py:697
  196.5 84.0 %all-to-all-start.3 = ((bf16[8,128,512]{2,1,0:T(8,128)(2,1)}), bf16[8,128,512]{2,1,0:T(8,128)(2,1)}, u32[]{:S(2)}, u32[]{:S(2)}) async-start(bf16[8,128,512]{2,1,0:T(8,128)(2,1)} %bitcast.65), calls=%async_computation.3 | async-start | bytes 2097152 | tf_op jit(solution)/shard_map/all_to_all | solution.py:653
  203.8 7.7 %collective-permute-start.7 = (bf16[16,16,1792]{2,1,0:T(8,128)(2,1)S(1)}, bf16[16,16,1792]{2,1,0:T(8,128)(2,1)S(1)}, u32[]{:S(2)}, u32[]{:S(2)}) collective-permute-start(bf16[16,16,1792]{2,1,0:T(8,128)(2,1)S(1)} %dynamic-slice_bitcast_fusion.1), channel_id=1, source_target_pairs={{0,1},{1,0},{2,3},{3,2},{4,5},{5,4},{6,7},{7,6},{8,9},{9,8},{10,11... | collective-permute-start | bytes 2752520 | tf_op jit(solution)/shard_map/ppermute | solution.py:697
  205.1 40.1 %collective-permute-start.24 = (bf16[4,16,4608]{2,1,0:T(8,128)(2,1)S(1)}, bf16[4,16,4608]{2,1,0:T(8,128)(2,1)S(1)}, u32[]{:S(2)}, u32[]{:S(2)}) collective-permute-start(bf16[4,16,4608]{2,1,0:T(8,128)(2,1)S(1)} %pad_maximum_fusion.1), channel_id=1, source_target_pairs={{0,4},{1,5},{2,6},{3,7},{4,0},{5,1},{6,2},{7,3},{8,12},{9,13},{10,... | collective-permute-start | bytes 1769480 | tf_op jit(solution)/shard_map/ppermute | solution.py:697
  207.2 50.0 %collective-permute-start.25 = (bf16[4,16,4608]{2,1,0:T(8,128)(2,1)S(1)}, bf16[4,16,4608]{2,1,0:T(8,128)(2,1)S(1)}, u32[]{:S(2)}, u32[]{:S(2)}) collective-permute-start(bf16[4,16,4608]{2,1,0:T(8,128)(2,1)S(1)} %pad_maximum_fusion.1), channel_id=1, source_target_pairs={{0,2},{1,3},{2,0},{3,1},{4,6},{5,7},{6,4},{7,5},{8,10},{9,11},{10,... | collective-permute-start | bytes 1769480 | tf_op jit(solution)/shard_map/ppermute | solution.py:697
  208.7 57.5 %collective-permute-start.26 = (bf16[4,16,4608]{2,1,0:T(8,128)(2,1)S(1)}, bf16[4,16,4608]{2,1,0:T(8,128)(2,1)S(1)}, u32[]{:S(2)}, u32[]{:S(2)}) collective-permute-start(bf16[4,16,4608]{2,1,0:T(8,128)(2,1)S(1)} %pad_maximum_fusion.1), channel_id=1, source_target_pairs={{0,6},{1,7},{2,4},{3,5},{4,2},{5,3},{6,0},{7,1},{8,14},{9,15},{10,... | collective-permute-start | bytes 1769480 | tf_op jit(solution)/shard_map/ppermute | solution.py:697
  212.1 33.2 %collective-permute-start.10 = (bf16[4,16,1792]{2,1,0:T(8,128)(2,1)S(1)}, bf16[4,16,1792]{2,1,0:T(8,128)(2,1)S(1)}, u32[]{:S(2)}, u32[]{:S(2)}) collective-permute-start(bf16[4,16,1792]{2,1,0:T(8,128)(2,1)S(1)} %get-tuple-element.93), channel_id=1, source_target_pairs={{0,6},{1,7},{2,4},{3,5},{4,2},{5,3},{6,0},{7,1},{8,14},{9,15},{10,... | collective-permute-start | bytes 688136 | tf_op jit(solution)/shard_map/ppermute | solution.py:697
  215.0 31.6 %collective-permute-start.9 = (bf16[4,16,1792]{2,1,0:T(8,128)(2,1)S(1)}, bf16[4,16,1792]{2,1,0:T(8,128)(2,1)S(1)}, u32[]{:S(2)}, u32[]{:S(2)}) collective-permute-start(bf16[4,16,1792]{2,1,0:T(8,128)(2,1)S(1)} %get-tuple-element.94), channel_id=1, source_target_pairs={{0,2},{1,3},{2,0},{3,1},{4,6},{5,7},{6,4},{7,5},{8,10},{9,11},{10,... | collective-permute-start | bytes 688136 | tf_op jit(solution)/shard_map/ppermute | solution.py:697
  245.2 7.0 %collective-permute-start.8 = (bf16[4,16,1792]{2,1,0:T(8,128)(2,1)S(1)}, bf16[4,16,1792]{2,1,0:T(8,128)(2,1)S(1)}, u32[]{:S(2)}, u32[]{:S(2)}) collective-permute-start(bf16[4,16,1792]{2,1,0:T(8,128)(2,1)S(1)} %get-tuple-element.92), channel_id=1, source_target_pairs={{0,4},{1,5},{2,6},{3,7},{4,0},{5,1},{6,2},{7,3},{8,12},{9,13},{10,... | collective-permute-start | bytes 688136 | tf_op jit(solution)/shard_map/ppermute | solution.py:697
  252.5 6.3 %collective-permute-start.13 = (bf16[1,16,1792]{2,1,0:T(8,128)(2,1)S(1)}, bf16[1,16,1792]{2,1,0:T(8,128)(2,1)S(1)}, u32[]{:S(2)}, u32[]{:S(2)}) collective-permute-start(bf16[1,16,1792]{2,1,0:T(8,128)(2,1)S(1)} %get-tuple-element.106), channel_id=1, source_target_pairs={{0,24},{1,25},{2,26},{3,27},{4,28},{5,29},{6,30},{7,31},{8,16},{9,... | collective-permute-start | bytes 172040 | tf_op jit(solution)/shard_map/ppermute | solution.py:697
  256.5 5.1 %collective-permute-start.12 = (bf16[1,16,1792]{2,1,0:T(8,128)(2,1)S(1)}, bf16[1,16,1792]{2,1,0:T(8,128)(2,1)S(1)}, u32[]{:S(2)}, u32[]{:S(2)}) collective-permute-start(bf16[1,16,1792]{2,1,0:T(8,128)(2,1)S(1)} %get-tuple-element.107), channel_id=1, source_target_pairs={{0,16},{1,17},{2,18},{3,19},{4,20},{5,21},{6,22},{7,23},{8,24},{9,... | collective-permute-start | bytes 172040 | tf_op jit(solution)/shard_map/ppermute | solution.py:697
  256.5 5.1 %collective-permute-start.11 = (bf16[1,16,1792]{2,1,0:T(8,128)(2,1)S(1)}, bf16[1,16,1792]{2,1,0:T(8,128)(2,1)S(1)}, u32[]{:S(2)}, u32[]{:S(2)}) collective-permute-start(bf16[1,16,1792]{2,1,0:T(8,128)(2,1)S(1)} %get-tuple-element.105), channel_id=1, source_target_pairs={{0,8},{1,9},{2,10},{3,11},{4,12},{5,13},{6,14},{7,15},{8,0},{9,1},... | collective-permute-start | bytes 172040 | tf_op jit(solution)/shard_map/ppermute | solution.py:697
  261.7 4.9 %collective-permute-start.14 = (bf16[1,16,1792]{2,1,0:T(8,128)(2,1)S(1)}, bf16[1,16,1792]{2,1,0:T(8,128)(2,1)S(1)}, u32[]{:S(2)}, u32[]{:S(2)}) collective-permute-start(bf16[1,16,1792]{2,1,0:T(8,128)(2,1)S(1)} %get-tuple-element.110), channel_id=1, source_target_pairs={{0,8},{1,9},{2,10},{3,11},{4,12},{5,13},{6,14},{7,15},{8,0},{9,1},... | collective-permute-start | bytes 172040 | tf_op jit(solution)/shard_map/ppermute | solution.py:697
  262.1 5.1 %collective-permute-start.15 = (bf16[1,16,1792]{2,1,0:T(8,128)(2,1)S(1)}, bf16[1,16,1792]{2,1,0:T(8,128)(2,1)S(1)}, u32[]{:S(2)}, u32[]{:S(2)}) collective-permute-start(bf16[1,16,1792]{2,1,0:T(8,128)(2,1)S(1)} %get-tuple-element.110), channel_id=1, source_target_pairs={{0,16},{1,17},{2,18},{3,19},{4,20},{5,21},{6,22},{7,23},{8,24},{9,... | collective-permute-start | bytes 172040 | tf_op jit(solution)/shard_map/ppermute | solution.py:697
  263.9 6.1 %collective-permute-start.16 = (bf16[1,16,1792]{2,1,0:T(8,128)(2,1)S(1)}, bf16[1,16,1792]{2,1,0:T(8,128)(2,1)S(1)}, u32[]{:S(2)}, u32[]{:S(2)}) collective-permute-start(bf16[1,16,1792]{2,1,0:T(8,128)(2,1)S(1)} %get-tuple-element.110), channel_id=1, source_target_pairs={{0,24},{1,25},{2,26},{3,27},{4,28},{5,29},{6,30},{7,31},{8,16},{9,... | collective-permute-start | bytes 172040 | tf_op jit(solution)/shard_map/ppermute | solution.py:697
  266.2 22.4 %collective-permute-start.27 = (bf16[16,16,4608]{2,1,0:T(8,128)(2,1)S(1)}, bf16[16,16,4608]{2,1,0:T(8,128)(2,1)}, u32[]{:S(2)}, u32[]{:S(2)}) collective-permute-start(bf16[16,16,4608]{2,1,0:T(8,128)(2,1)S(1)} %constant_dynamic-update-slice_fusion.7.own_ref), channel_id=1, source_target_pairs={{0,1},{1,0},{2,3},{3,2},{4,5},{5,4},{6,7},{7,6},{8,9},{9,8},{10,11... | collective-permute-start | bytes 7077896 | tf_op jit(solution)/shard_map/ppermute | solution.py:697
  270.0 8.0 %collective-permute-start.17 = (bf16[4,16,1792]{2,1,0:T(8,128)(2,1)S(1)}, bf16[4,16,1792]{2,1,0:T(8,128)(2,1)S(1)}, u32[]{:S(2)}, u32[]{:S(2)}) collective-permute-start(bf16[4,16,1792]{2,1,0:T(8,128)(2,1)S(1)} %pad_maximum_fusion.3), channel_id=1, source_target_pairs={{0,4},{1,5},{2,6},{3,7},{4,0},{5,1},{6,2},{7,3},{8,12},{9,13},{10,... | collective-permute-start | bytes 688136 | tf_op jit(solution)/shard_map/ppermute | solution.py:697
  270.4 7.6 %collective-permute-start.18 = (bf16[4,16,1792]{2,1,0:T(8,128)(2,1)S(1)}, bf16[4,16,1792]{2,1,0:T(8,128)(2,1)S(1)}, u32[]{:S(2)}, u32[]{:S(2)}) collective-permute-start(bf16[4,16,1792]{2,1,0:T(8,128)(2,1)S(1)} %pad_maximum_fusion.3), channel_id=1, source_target_pairs={{0,2},{1,3},{2,0},{3,1},{4,6},{5,7},{6,4},{7,5},{8,10},{9,11},{10,... | collective-permute-start | bytes 688136 | tf_op jit(solution)/shard_map/ppermute | solution.py:697
  271.9 8.6 %collective-permute-start.19 = (bf16[4,16,1792]{2,1,0:T(8,128)(2,1)S(1)}, bf16[4,16,1792]{2,1,0:T(8,128)(2,1)S(1)}, u32[]{:S(2)}, u32[]{:S(2)}) collective-permute-start(bf16[4,16,1792]{2,1,0:T(8,128)(2,1)S(1)} %pad_maximum_fusion.3), channel_id=1, source_target_pairs={{0,6},{1,7},{2,4},{3,5},{4,2},{5,3},{6,0},{7,1},{8,14},{9,15},{10,... | collective-permute-start | bytes 688136 | tf_op jit(solution)/shard_map/ppermute | solution.py:697
  280.5 2.7 collective-permute-start.20
  (31 other events, 336.5 us)
